TPU v7x, 32 devices: a whole 2x2x4 slice. The times are simulated.
32 devices in a mesh: parts: 2 (over y), tok: 8 (over z, x), layer: 2 (over core).
Axes of the slice: x: 2, y: 2, z: 4, core: 2. Of those that a mesh axis runs over, the one named last changes fastest.
Arguments:
- hidden_in: bfloat16 [2, 2560, 11008], P('layer', ('parts', 'tok')), parts along dimension 1, may hold values from -6 to 6
- grad_out: bfloat16 [2, 2560, 4096], P('layer', ('parts', 'tok')), parts along dimension 1, may hold values from -6 to 6
- layer_ids: int32 [32], replicated, may hold values from 0 to 31, each once
- factor_in: bfloat16 [32, 11008, 128], P(None, 'tok'), may hold values from -0.0546875 to 0.0546875
- factor_out: bfloat16 [32, 4096, 128], P(None, 'tok'), may hold values from -0.09375 to 0.09375
Outputs:
- influence: float32 [2560, 32], P(('parts', 'tok', 'layer')), parts along dimension 0
There are 2 independent parts, one for each index of `parts`. A program takes and returns all parts, laid end to end along the dimension named above; an argument that names none is the same for every part. Nothing has to cross between parts.
Inputs may be any that keep to these rules, and one draw needn't show every extreme that they name: `layer_ids`: each of the 32 model layers appears exactly once.
All inputs are finite; a program needn't handle non-finite values.
Results may differ from a plain program's by a relative error of at most 0.0003.
Values may be sent and summed in bfloat16 or wider, within the bound.
No kernel may reach another device: no remote copies, remote signals or barrier semaphores. Data moves between devices by JAX's collectives and lax.ppermute only.
A program may use at most 64 MiB of HBM per device.

v0:
```python
import jax
import jax.numpy as jnp
from jax import lax
from jax.sharding import PartitionSpec as P

QUERIES = 32
RANK = 4


def per_device(hidden_in, grad_out, layer_ids, factor_in, factor_out):
    slot_index = lax.axis_index("layer") * hidden_in.shape[0]
    chosen = lax.dynamic_index_in_dim(layer_ids, slot_index, 0, keepdims=False)
    my_inward = lax.dynamic_index_in_dim(factor_in, chosen, 0, keepdims=False)
    my_outward = lax.dynamic_index_in_dim(factor_out, chosen, 0, keepdims=False)
    hidden_rows = hidden_in[0]
    grad_rows = grad_out[0]
    row_count = hidden_rows.shape[0]
    full_inward, full_outward = (
        lax.all_gather(my_inward, "tok", axis=0, tiled=True),
        lax.all_gather(my_outward, "tok", axis=0, tiled=True),
    )
    in_proj = jnp.dot(hidden_rows, full_inward, preferred_element_type=jnp.float32)
    out_proj = jnp.dot(grad_rows, full_outward, preferred_element_type=jnp.float32)
    joined = in_proj * out_proj
    scores = joined.reshape(row_count, QUERIES, RANK).sum(axis=2)
    summed = lax.psum(scores, "layer")
    halves = row_count // lax.axis_size("layer")
    return lax.dynamic_slice_in_dim(summed, lax.axis_index("layer") * halves, halves, 0)


def solution(mesh):
    in_specs = (
        P("layer", ("parts", "tok"), None),
        P("layer", ("parts", "tok"), None),
        P(),
        P(None, "tok", None),
        P(None, "tok", None),
    )
    out_specs = P(("parts", "tok", "layer"), None)
    return jax.shard_map(
        per_device, mesh=mesh, in_specs=in_specs, out_specs=out_specs, check_vma=False
    )
```

profile of v0, /device:TPU:0, one launch (start us, length us, event | category | flops | bytes accessed | tf_op | source)
XLA Modules:
  0.0 131.7 jit_solution(16068410267480362368)
XLA Ops:
  6.5 0.0 copy-start
  6.5 0.0 all-gather.5.cloned.1.call-start
  6.5 1.4 %dynamic_slice.15 = s32[1]{0:T(128)} dynamic-slice(s32[32]{0:T(128)} %param.7, s32[]{:T(128)S(6)} %select_n.13), dynamic_slice_sizes={1} | dynamic-slice | bytes 12 | tf_op jit(solution)/shard_map/jit(dynamic_index_in_dim)/dynamic_slice | solution.py:12
  9.9 1.7 %constant_dynamic-slice_fusion.2 = bf16[1,1376,128]{2,1,0:T(8,128)(2,1)} fusion(bf16[32,1376,128]{2,1,0:T(8,128)(2,1)} %param.8, s32[]{:T(128)S(6)} %select_n.14), kind=kLoop, calls=%fused_computation.10 | loop fusion | bytes 704516 | tf_op jit(solution)/shard_map/jit(dynamic_index_in_dim)/dynamic_slice | solution.py:13
  11.6 0.0 all-gather.5.cloned.1.call-update
  11.6 0.0 all-gather.7.cloned.1.call-start
  11.7 1.6 %constant_dynamic-slice_fusion.1 = bf16[1,512,128]{2,1,0:T(8,128)(2,1)} fusion(bf16[32,512,128]{2,1,0:T(8,128)(2,1)} %param.9, s32[]{:T(128)S(6)} %select_n.14), kind=kLoop, calls=%fused_computation.9 | loop fusion | bytes 262148 | tf_op jit(solution)/shard_map/jit(dynamic_index_in_dim)/dynamic_slice | solution.py:14
  13.3 0.0 all-gather.7.cloned.1.call-update
  13.3 58.2 %all-gather.5.cloned.1.call-done = bf16[1,11008,128]{2,1,0:T(8,128)(2,1)} async-done(((bf16[1,1376,128]{2,1,0:T(8,128)(2,1)}), bf16[1,11008,128]{2,1,0:T(8,128)(2,1)}) %all-gather.5.cloned.1.call-update) | async-done | bytes 2818064 | tf_op jit(solution)/shard_map/all_gather | solution.py:19
  71.5 0.0 copy-done
  71.5 3.5 %fusion = f32[128,160]{0,1:T(8,128)} fusion(bf16[1,160,11008]{2,1,0:T(8,128)(2,1)S(1)} %copy-done, bf16[1,11008,128]{2,1,0:T(8,128)(2,1)} %all-gather.5.cloned.1.call-done), kind=kOutput, calls=%fused_computation | convolution fusion | flops 450887680 | bytes 6422528 | tf_op jit(solution)/shard_map/dot_general | solution.py:22
  75.0 37.5 %all-gather.7.cloned.1.call-done = bf16[1,4096,128]{2,1,0:T(8,128)(2,1)} async-done(((bf16[1,512,128]{2,1,0:T(8,128)(2,1)}), bf16[1,4096,128]{2,1,0:T(8,128)(2,1)}) %all-gather.7.cloned.1.call-update) | async-done | bytes 1048592 | tf_op jit(solution)/shard_map/all_gather | solution.py:20
  112.4 2.8 %fusion.8 = f32[160,128]{1,0:T(8,128)} fusion(f32[128,160]{0,1:T(8,128)} %fusion, bf16[1,160,4096]{2,1,0:T(8,128)(2,1)} %param.6, bf16[1,4096,128]{2,1,0:T(8,128)(2,1)} %all-gather.7.cloned.1.call-done), kind=kOutput, calls=%fused_computation.6 | convolution fusion | flops 167792640 | bytes 2523136 | tf_op jit(solution)/shard_map/dot_general | solution.py:23
  115.2 1.6 %copy.6 = f32[160,128]{0,1:T(8,128)} copy(f32[160,128]{1,0:T(8,128)} %fusion.8) | data formatting | bytes 163840 | tf_op jit(solution)/shard_map/mul | solution.py:24
  116.8 1.6 %reshape.3 = f32[160,32,4]{0,2,1:T(4,128)} reshape(f32[160,128]{0,1:T(8,128)} %copy.6) | data formatting | bytes 163840 | tf_op jit(solution)/shard_map/reshape | solution.py:25
  118.4 1.0 reduce_sum.9
  119.4 4.0 %psum.7 = f32[160,32]{0,1:T(8,128)} all-reduce(f32[160,32]{0,1:T(8,128)S(1)} %reduce_sum.9), channel_id=1, replica_groups=mesh['parts'=2,'tok'=8,'layer'=2] {'layer'}, use_global_device_ids=true, to_apply=%region_1.2 | all-reduce | flops 5120 | bytes 40960 | tf_op jit(solution)/shard_map/psum | solution.py:26
  123.4 1.4 %constant_dynamic-slice_fusion = f32[80,32]{0,1:T(8,128)} fusion(f32[160,32]{0,1:T(8,128)} %psum.7, s32[]{:T(128)S(6)} %select_n.15), kind=kLoop, calls=%fused_computation.8 | loop fusion | bytes 20484 | tf_op jit(solution)/shard_map/dynamic_slice | solution.py:28
Async XLA Ops:
  6.5 64.9 %copy-start = (bf16[1,160,11008]{2,1,0:T(8,128)(2,1)S(1)}, bf16[1,160,11008]{2,1,0:T(8,128)(2,1)}, u32[]{:S(2)}) copy-start(bf16[1,160,11008]{2,1,0:T(8,128)(2,1)} %param.5) | copy-start | bytes 10567684
  6.5 64.9 %all-gather.5.cloned.1.call-start = ((), (), s32[]{:S(2)}) async-start(), calls=%async_computation | async-start | bytes 3170304 | tf_op jit(solution)/shard_map/all_gather | solution.py:19
  11.6 100.8 %all-gather.7.cloned.1.call-start = ((), (), s32[]{:S(2)}) async-start(), calls=%async_computation.1 | async-start | bytes 1179648 | tf_op jit(solution)/shard_map/all_gather | solution.py:20
Sparse Core Ops, SparseCore 0:
  11.8 59.6 all-gather.4
  73.6 38.8 all-gather.6
where the time goes:
time: 132 us
  waiting for transfers between devices  95.7 us (72%)
  between operations  15.4 us (12%)
  local copies, waits for them, and re-layouts  9.34 us (7%)
  matrix products  6.26 us (5%)
  blocking collectives  3.99 us (3%)
    all_gather x1, waiting for transfers between devices, per_device(): lax.all_gather(my_inward, 'tok', axis=0, tiled=True)  58.2 us
    all_gather x1, waiting for transfers between devices, per_device(): lax.all_gather(my_outward, 'tok', axis=0, tiled=True)  37.5 us
    psum x1, blocking collectives, per_device(): summed = lax.psum(scores, 'layer')  3.99 us
    dot_general x1, matrix products, per_device(): jnp.dot(hidden_rows, full_inward, preferred_element_type=jnp.float32)  3.5 us
    dot_general x1, matrix products, per_device(): jnp.dot(grad_rows, full_outward, preferred_element_type=jnp.float32)  2.76 us
  transfers between devices with their start and end apart: 2, of which 2 were waited for; matrix products, arithmetic and copies ran while one was open for 4% of the time, Pallas kernels for 0%

commit v1 on v0

--- a/solution.py
+++ b/solution.py
@@ -1,13 +1,19 @@
+import functools
+
 import jax
 import jax.numpy as jnp
 from jax import lax
+from jax.experimental import pallas as pl
+from jax.experimental.pallas import tpu as pltpu
 from jax.sharding import PartitionSpec as P
 
 QUERIES = 32
 RANK = 4
-
-
-def per_device(hidden_in, grad_out, layer_ids, factor_in, factor_out):
+AXES = ("parts", "tok", "layer")
+LANES = 128
+
+
+def gathered_form(hidden_in, grad_out, layer_ids, factor_in, factor_out):
     slot_index = lax.axis_index("layer") * hidden_in.shape[0]
     chosen = lax.dynamic_index_in_dim(layer_ids, slot_index, 0, keepdims=False)
     my_inward = lax.dynamic_index_in_dim(factor_in, chosen, 0, keepdims=False)
@@ -28,6 +34,170 @@
     return lax.dynamic_slice_in_dim(summed, lax.axis_index("layer") * halves, halves, 0)
 
 
+def take_halves(half, ids_ref, in_ref, out_ref, own_ref, other_ref, sems):
+    chosen = ids_ref[lax.axis_index("layer")]
+    part = lax.axis_index("parts")
+    tail = in_ref.shape[1] - half
+
+    def run(first_ref, second_ref):
+        copies = (
+            pltpu.make_async_copy(in_ref.at[chosen, pl.ds(0, half)], first_ref, sems.at[0]),
+            pltpu.make_async_copy(in_ref.at[chosen, pl.ds(half, tail)], second_ref.at[pl.ds(0, tail)], sems.at[1]),
+            pltpu.make_async_copy(out_ref.at[chosen], second_ref.at[pl.ds(tail, half - tail)], sems.at[2]),
+        )
+        for copy in copies:
+            copy.start()
+        for copy in copies:
+            copy.wait()
+
+    pl.when(part == 0)(lambda: run(own_ref, other_ref))
+    pl.when(part == 1)(lambda: run(other_ref, own_ref))
+
+
+def add_blocks(offsets, in_rows, half, hidden_ref, grad_ref, pieces, window, acc_in, acc_out):
+    part = lax.axis_index("parts")
+    tok = lax.axis_index("tok")
+    span = window.shape[1]
+    tail = in_rows - half
+    out_rows = half - tail
+    for i, offset in enumerate(offsets):
+        own_ref, other_ref = pieces[2 * i], pieces[2 * i + 1]
+        source = tok ^ offset
+        row = source * in_rows
+        start = jnp.minimum(row // LANES * LANES, hidden_ref.shape[1] - span)
+        shift = pl.multiple_of(row - start, 32)
+        window[i] = jnp.zeros((span, LANES), jnp.bfloat16)
+
+        def place(first_ref, second_ref):
+            window[i, pl.ds(shift, half), :] = first_ref[...]
+            window[i, pl.ds(pl.multiple_of(shift + half, 16), tail), :] = second_ref[:tail, :]
+
+        pl.when(part == 0)(lambda: place(own_ref, other_ref))
+        pl.when(part == 1)(lambda: place(other_ref, own_ref))
+        outward = jnp.where(part == 0, other_ref[tail:, :], own_ref[tail:, :])
+        acc_in = acc_in + jnp.dot(
+            hidden_ref[:, pl.ds(pl.multiple_of(start, LANES), span)], window[i], preferred_element_type=jnp.float32
+        )
+        acc_out = acc_out + jnp.dot(
+            grad_ref[:, pl.ds(pl.multiple_of(source * out_rows, LANES), out_rows)], outward,
+            preferred_element_type=jnp.float32,
+        )
+    return acc_in, acc_out
+
+
+def early(offsets, in_rows, half, hidden_ref, grad_ref, *refs):
+    pieces, (in_ref, out_ref, window) = refs[:-3], refs[-3:]
+    zero = jnp.zeros(in_ref.shape, jnp.float32)
+    in_ref[...], out_ref[...] = add_blocks(
+        offsets, in_rows, half, hidden_ref, grad_ref, pieces, window, zero, zero
+    )
+
+
+def late(offsets, in_rows, half, hidden_ref, grad_ref, in_ref, out_ref, *refs):
+    pieces, (kept_ref, sent_ref, window) = refs[:-3], refs[-3:]
+    in_proj, out_proj = add_blocks(
+        offsets, in_rows, half, hidden_ref, grad_ref, pieces, window, in_ref[...], out_ref[...]
+    )
+    joined = in_proj * out_proj
+    lane = lax.broadcasted_iota(jnp.int32, (QUERIES, LANES), 1)
+    query = lax.broadcasted_iota(jnp.int32, (QUERIES, LANES), 0)
+    groups = (lane // RANK == query).astype(jnp.float32)
+    scores = [
+        lax.dot_general(
+            groups, rows, (((1,), (1,)), ((), ())), precision=lax.Precision.HIGHEST,
+            preferred_element_type=jnp.float32,
+        )
+        for rows in jnp.split(joined, 2, axis=0)
+    ]
+    first = lax.axis_index("layer") == 0
+    kept_ref[...] = jnp.where(first, scores[0], scores[1])
+    sent_ref[...] = jnp.where(first, scores[1], scores[0])
+
+
+def swapped_form(x_size, hidden_in, grad_out, layer_ids, factor_in, factor_out):
+    parts, toks, layers = (lax.axis_size(a) for a in AXES)
+    in_rows, out_rows = factor_in.shape[1], factor_out.shape[1]
+    half = (in_rows + out_rows) // 2
+    rows = hidden_in.shape[1]
+    hidden, grad = hidden_in[0], grad_out[0]
+    vmem = pl.BlockSpec(memory_space=pltpu.VMEM)
+
+    def swap(value, part=0, tok=0, layer=0):
+        def index(p, t, c):
+            return (p * toks + t) * layers + c
+
+        pairs = [
+            (index(p, t, c), index(p ^ part, t ^ tok, c ^ layer))
+            for p in range(parts) for t in range(toks) for c in range(layers)
+        ]
+        return lax.ppermute(value, AXES, pairs)
+
+    across_x = functools.partial(swap, tok=1)
+    across_y = functools.partial(swap, part=1)
+    z_one = functools.partial(swap, tok=x_size)
+    z_two = functools.partial(swap, tok=2 * x_size)
+
+    piece = jax.ShapeDtypeStruct((half, LANES), jnp.bfloat16)
+    own, other = pl.pallas_call(
+        functools.partial(take_halves, half),
+        out_shape=(piece, piece),
+        in_specs=[pl.BlockSpec(memory_space=pltpu.SMEM)] + [pl.BlockSpec(memory_space=pl.ANY)] * 2,
+        out_specs=[vmem] * 2,
+        scratch_shapes=[pltpu.SemaphoreType.DMA((3,))],
+    )(layer_ids, factor_in, factor_out)
+
+    z1, z2, x0 = z_one(own), z_two(own), across_x(own)
+    z1_other = z_one(other)
+    y0 = across_y(x0)
+    x1, x2, y2 = across_x(z1), across_x(z2), across_y(z2)
+    z3 = z_one(z2)
+    x3, y3 = across_x(z3), across_y(z3)
+    y1, y2x = across_y(x1), across_y(x2)
+    x3y = across_x(y3)
+
+    def cost(blocks):
+        return pl.CostEstimate(
+            flops=2 * rows * LANES * (in_rows + out_rows) * blocks,
+            bytes_accessed=2 * (rows + LANES) * (in_rows + out_rows) * blocks, transcendentals=0,
+        )
+
+    span = -(-(in_rows + LANES) // LANES) * LANES
+    total = jax.ShapeDtypeStruct((rows, LANES), jnp.float32)
+
+    def window(blocks):
+        return pltpu.VMEM((blocks, span, LANES), jnp.bfloat16)
+
+    near = (0, 1, x_size, 2 * x_size)
+    sums = pl.pallas_call(
+        functools.partial(early, near, in_rows, half),
+        out_shape=(total, total),
+        in_specs=[vmem] * 10,
+        out_specs=[vmem] * 2,
+        scratch_shapes=[window(4)],
+        cost_estimate=cost(4),
+        compiler_params=pltpu.CompilerParams(vmem_limit_bytes=24 << 20),
+    )(hidden, grad, own, other, x0, y0, z1, z1_other, z2, y2)
+    far = (x_size + 1, 2 * x_size + 1, 3 * x_size, 3 * x_size + 1)
+    score = jax.ShapeDtypeStruct((QUERIES, rows // 2), jnp.float32)
+    kept, sent = pl.pallas_call(
+        functools.partial(late, far, in_rows, half),
+        out_shape=(score, score),
+        in_specs=[vmem] * 12,
+        out_specs=[vmem] * 2,
+        scratch_shapes=[window(4)],
+        cost_estimate=cost(4),
+        compiler_params=pltpu.CompilerParams(vmem_limit_bytes=24 << 20),
+    )(hidden, grad, *sums, x1, y1, x2, y2x, z3, y3, x3, x3y)
+    return (kept + swap(sent, layer=1)).T
+
+
+def x_chips(mesh):
+    places = [getattr(d, "coords", None) for d in mesh.devices[0, :, 0]]
+    if any(p is None for p in places):
+        return 0
+    return len({p[0] for p in places})
+
+
 def solution(mesh):
     in_specs = (
         P("layer", ("parts", "tok"), None),
@@ -37,6 +207,9 @@
         P(None, "tok", None),
     )
     out_specs = P(("parts", "tok", "layer"), None)
+    x_size = x_chips(mesh)
+    small = tuple(mesh.shape[a] for a in AXES) == (2, 8, 2) and x_size == 2
+    form = functools.partial(swapped_form, x_size) if small else gathered_form
     return jax.shard_map(
-        per_device, mesh=mesh, in_specs=in_specs, out_specs=out_specs, check_vma=False
-    )
+        form, mesh=mesh, in_specs=in_specs, out_specs=out_specs, check_vma=False
+    )

time: 132 us -> 52.7 us (0.40)
  waiting for transfers between devices: 95.7 us -> 21.7 us
  starting transfers between devices: 0.04 us -> 20.7 us
  between operations: 15.4 us -> 0.06 us
  matrix products: 6.26 us -> 0 us
  Pallas kernels: 0 us -> 6.18 us
  local copies, waits for them, and re-layouts: 9.34 us -> 3.2 us
  blocking collectives: 3.99 us -> 0 us
    all_gather x2 -> x0, waiting for transfers between devices: 95.7 us -> none  [the longest x1 58.2 us: per_device(): lax.all_gather(my_inward, 'tok', axis=0, tiled=True)]
    ppermute x0 -> x15, waiting for transfers between devices: none -> 21.7 us  [swap(): return lax.ppermute(value, AXES, pairs)]
    ppermute x0 -> x15, starting transfers between devices: none -> 20.7 us  [swap(): return lax.ppermute(value, AXES, pairs)]
    dot_general x2 -> x0, matrix products: 6.26 us -> none  [the longest x1 3.5 us: per_device(): jnp.dot(hidden_rows, full_inward, preferred_element_type=jnp.float32)]
    pallas_call x0 -> x3, Pallas kernels: none -> 6.18 us  [the longest x1 2.94 us: swapped_form(): pl.pallas_call(functools.partial(take_halves, half), out_shape=(piece, pi...]
    dynamic_slice x4 -> x0, local copies, waits for them, and re-layouts: 6.13 us -> none  [the longest x1 1.74 us: per_device(): my_inward = lax.dynamic_index_in_dim(factor_in, chosen, 0, keepdims=False)]
    psum x1 -> x0, blocking collectives: 3.99 us -> none  [per_device(): summed = lax.psum(scores, 'layer')]
    unnamed x2 -> x8, local copies, waits for them, and re-layouts: 0.01 us -> 3.2 us
  transfers between devices with their start and end apart: 2 -> 15, of which waited for: 2 -> 7; matrix products, arithmetic and copies ran while one was open for 4% -> 0% of each run, Pallas kernels for 0% -> 3%
where the time goes in v1:
time: 52.7 us; the launch traced here: 52.4 us
  waiting for transfers between devices  21.7 us (41%)
  starting transfers between devices  20.7 us (39%)
  Pallas kernels  6.18 us (12%)
  local copies, waits for them, and re-layouts  3.2 us (6%)
  other arithmetic  0.61 us (1%)
    ppermute x15, waiting for transfers between devices, swap(): return lax.ppermute(value, AXES, pairs)  21.7 us
    ppermute x15, starting transfers between devices, swap(): return lax.ppermute(value, AXES, pairs)  20.7 us
    unnamed x8, local copies, waits for them, and re-layouts  3.2 us
    pallas_call x1, Pallas kernels, swapped_form(): pl.pallas_call(functools.partial(take_halves, half), out_shape=(piece, pi...  2.94 us
    pallas_call x1, Pallas kernels, swapped_form(): pl.pallas_call(functools.partial(late, far, in_rows, half), out_shape=(sc...  1.7 us
    pallas_call x1, Pallas kernels, swapped_form(): pl.pallas_call(functools.partial(early, near, in_rows, half), out_shape=(...  1.55 us
  transfers between devices with their start and end apart: 15, of which 7 were waited for; matrix products, arithmetic and copies ran while one was open for 0% of the time, Pallas kernels for 3%

profile of v1, /device:TPU:0, one launch (start us, length us, event | category | flops | bytes accessed | tf_op | source)
XLA Modules:
  0.0 52.4 jit_solution(15126471144388080361)
XLA Ops:
  0.0 2.9 %shard_map.55 = (bf16[944,128]{1,0:T(8,128)(2,1)}, bf16[944,128]{1,0:T(8,128)(2,1)}) custom-call(s32[32]{0:T(128)} %ids_ref.1, bf16[32,1376,128]{2,1,0:T(8,128)(2,1)} %in_ref.1, bf16[32,512,128]{2,1,0:T(8,128)(2,1)} %out_ref.1), custom_call_target="tpu_custom_call" | custom-call | tf_op jit(solution)/shard_map/pallas_call | solution.py:141
  3.0 4.1 %collective-permute-start.4 = (bf16[944,128]{1,0:T(8,128)(2,1)}, bf16[944,128]{1,0:T(8,128)(2,1)S(1)}, u32[]{:S(2)}, u32[]{:S(2)}) collective-permute-start(bf16[944,128]{1,0:T(8,128)(2,1)} %get-tuple-element.11.refs_0_), channel_id=1, source_target_pairs={{0,8},{1,9},{2,10},{3,11},{4,12},{5,13},{6,14},{7,15},{8,0},{9,1},... | collective-permute-start | bytes 725000 | tf_op jit(solution)/shard_map/ppermute | solution.py:133
  7.1 1.5 %collective-permute-start = (bf16[944,128]{1,0:T(8,128)(2,1)}, bf16[944,128]{1,0:T(8,128)(2,1)S(1)}, u32[]{:S(2)}, u32[]{:S(2)}) collective-permute-start(bf16[944,128]{1,0:T(8,128)(2,1)} %get-tuple-element.11.refs_0_), channel_id=1, source_target_pairs={{0,2},{1,3},{2,0},{3,1},{4,6},{5,7},{6,4},{7,5},{8,10},{9,11},{10,... | collective-permute-start | bytes 725000 | tf_op jit(solution)/shard_map/ppermute | solution.py:133
  8.5 1.6 %collective-permute-start.2 = (bf16[944,128]{1,0:T(8,128)(2,1)}, bf16[944,128]{1,0:T(8,128)(2,1)S(1)}, u32[]{:S(2)}, u32[]{:S(2)}) collective-permute-start(bf16[944,128]{1,0:T(8,128)(2,1)} %get-tuple-element.11.refs_0_), channel_id=1, source_target_pairs={{0,4},{1,5},{2,6},{3,7},{4,0},{5,1},{6,2},{7,3},{8,12},{9,13},{10,... | collective-permute-start | bytes 725000 | tf_op jit(solution)/shard_map/ppermute | solution.py:133
  10.1 8.3 %collective-permute-done.4.refs_6_ = bf16[944,128]{1,0:T(8,128)(2,1)S(1)} collective-permute-done((bf16[944,128]{1,0:T(8,128)(2,1)}, bf16[944,128]{1,0:T(8,128)(2,1)S(1)}, u32[]{:S(2)}, u32[]{:S(2)}) %collective-permute-start.4) | collective-permute-done | bytes 241696 | tf_op jit(solution)/shard_map/ppermute | solution.py:133
  18.4 0.8 %collective-permute-start.10 = (bf16[944,128]{1,0:T(8,128)(2,1)S(1)}, bf16[944,128]{1,0:T(8,128)(2,1)S(1)}, u32[]{:S(2)}, u32[]{:S(2)}) collective-permute-start(bf16[944,128]{1,0:T(8,128)(2,1)S(1)} %collective-permute-done.4.refs_6_), channel_id=1, source_target_pairs={{0,4},{1,5},{2,6},{3,7},{4,0},{5,1},{6,2},{7,3},{8,12},{9,13},{10,... | collective-permute-start | bytes 725000 | tf_op jit(solution)/shard_map/ppermute | solution.py:133
  19.2 1.3 %collective-permute-start.3 = (bf16[944,128]{1,0:T(8,128)(2,1)}, bf16[944,128]{1,0:T(8,128)(2,1)S(1)}, u32[]{:S(2)}, u32[]{:S(2)}) collective-permute-start(bf16[944,128]{1,0:T(8,128)(2,1)} %get-tuple-element.12.refs_1_), channel_id=1, source_target_pairs={{0,4},{1,5},{2,6},{3,7},{4,0},{5,1},{6,2},{7,3},{8,12},{9,13},{10,... | collective-permute-start | bytes 725000 | tf_op jit(solution)/shard_map/ppermute | solution.py:133
  20.4 1.6 %collective-permute-start.5 = (bf16[944,128]{1,0:T(8,128)(2,1)S(1)}, bf16[944,128]{1,0:T(8,128)(2,1)S(1)}, u32[]{:S(2)}, u32[]{:S(2)}) collective-permute-start(bf16[944,128]{1,0:T(8,128)(2,1)S(1)} %collective-permute-done.4.refs_6_), channel_id=1, source_target_pairs={{0,16},{1,17},{2,18},{3,19},{4,20},{5,21},{6,22},{7,23},{8,24},{9,... | collective-permute-start | bytes 725000 | tf_op jit(solution)/shard_map/ppermute | solution.py:133
  22.0 0.0 collective-permute-done.refs_2_
  22.0 1.5 %collective-permute-start.8 = (bf16[944,128]{1,0:T(8,128)(2,1)S(1)}, bf16[944,128]{1,0:T(8,128)(2,1)S(1)}, u32[]{:S(2)}, u32[]{:S(2)}) collective-permute-start(bf16[944,128]{1,0:T(8,128)(2,1)S(1)} %collective-permute-done.4.refs_6_), channel_id=1, source_target_pairs={{0,2},{1,3},{2,0},{3,1},{4,6},{5,7},{6,4},{7,5},{8,10},{9,11},{10,... | collective-permute-start | bytes 725000 | tf_op jit(solution)/shard_map/ppermute | solution.py:133
  23.5 0.0 collective-permute-done.2.refs_4_
  23.5 0.5 %collective-permute-start.6 = (bf16[944,128]{1,0:T(8,128)(2,1)S(1)}, bf16[944,128]{1,0:T(8,128)(2,1)S(1)}, u32[]{:S(2)}, u32[]{:S(2)}) collective-permute-start(bf16[944,128]{1,0:T(8,128)(2,1)S(1)} %collective-permute-done.2.refs_4_), channel_id=1, source_target_pairs={{0,2},{1,3},{2,0},{3,1},{4,6},{5,7},{6,4},{7,5},{8,10},{9,11},{10,... | collective-permute-start | bytes 725000 | tf_op jit(solution)/shard_map/ppermute | solution.py:133
  24.1 3.2 %collective-permute-done.10.refs_4_ = bf16[944,128]{1,0:T(8,128)(2,1)S(1)} collective-permute-done((bf16[944,128]{1,0:T(8,128)(2,1)S(1)}, bf16[944,128]{1,0:T(8,128)(2,1)S(1)}, u32[]{:S(2)}, u32[]{:S(2)}) %collective-permute-start.10) | collective-permute-done | bytes 241696 | tf_op jit(solution)/shard_map/ppermute | solution.py:133
  27.2 1.6 %collective-permute-start.11 = (bf16[944,128]{1,0:T(8,128)(2,1)S(1)}, bf16[944,128]{1,0:T(8,128)(2,1)S(1)}, u32[]{:S(2)}, u32[]{:S(2)}) collective-permute-start(bf16[944,128]{1,0:T(8,128)(2,1)S(1)} %collective-permute-done.10.refs_4_), channel_id=1, source_target_pairs={{0,16},{1,17},{2,18},{3,19},{4,20},{5,21},{6,22},{7,23},{8,24},{9,... | collective-permute-start | bytes 725000 | tf_op jit(solution)/shard_map/ppermute | solution.py:133
  28.8 1.8 %collective-permute-done.3.refs_5_ = bf16[944,128]{1,0:T(8,128)(2,1)S(1)} collective-permute-done((bf16[944,128]{1,0:T(8,128)(2,1)}, bf16[944,128]{1,0:T(8,128)(2,1)S(1)}, u32[]{:S(2)}, u32[]{:S(2)}) %collective-permute-start.3) | collective-permute-done | bytes 241696 | tf_op jit(solution)/shard_map/ppermute | solution.py:133
  30.6 1.3 %collective-permute-start.1 = (bf16[944,128]{1,0:T(8,128)(2,1)S(1)}, bf16[944,128]{1,0:T(8,128)(2,1)S(1)}, u32[]{:S(2)}, u32[]{:S(2)}) collective-permute-start(bf16[944,128]{1,0:T(8,128)(2,1)S(1)} %collective-permute-done.refs_2_), channel_id=1, source_target_pairs={{0,16},{1,17},{2,18},{3,19},{4,20},{5,21},{6,22},{7,23},{8,24},{9,... | collective-permute-start | bytes 725000 | tf_op jit(solution)/shard_map/ppermute | solution.py:133
  31.9 1.4 %collective-permute-start.12 = (bf16[944,128]{1,0:T(8,128)(2,1)S(1)}, bf16[944,128]{1,0:T(8,128)(2,1)S(1)}, u32[]{:S(2)}, u32[]{:S(2)}) collective-permute-start(bf16[944,128]{1,0:T(8,128)(2,1)S(1)} %collective-permute-done.10.refs_4_), channel_id=1, source_target_pairs={{0,2},{1,3},{2,0},{3,1},{4,6},{5,7},{6,4},{7,5},{8,10},{9,11},{10,... | collective-permute-start | bytes 725000 | tf_op jit(solution)/shard_map/ppermute | solution.py:133
  33.4 0.0 collective-permute-done.8.refs_2_
  33.4 0.5 collective-permute-start.9
  33.9 1.5 %collective-permute-start.7 = (bf16[944,128]{1,0:T(8,128)(2,1)S(1)}, bf16[944,128]{1,0:T(8,128)(2,1)S(1)}, u32[]{:S(2)}, u32[]{:S(2)}) collective-permute-start(bf16[944,128]{1,0:T(8,128)(2,1)S(1)} %collective-permute-done.6.refs_0_), channel_id=1, source_target_pairs={{0,16},{1,17},{2,18},{3,19},{4,20},{5,21},{6,22},{7,23},{8,24},{9,... | collective-permute-start | bytes 725000 | tf_op jit(solution)/shard_map/ppermute | solution.py:133
  35.4 1.5 %collective-permute-start.13 = (bf16[944,128]{1,0:T(8,128)(2,1)S(1)}, bf16[944,128]{1,0:T(8,128)(2,1)S(1)}, u32[]{:S(2)}, u32[]{:S(2)}) collective-permute-start(bf16[944,128]{1,0:T(8,128)(2,1)S(1)} %collective-permute-done.11.refs_5_), channel_id=1, source_target_pairs={{0,2},{1,3},{2,0},{3,1},{4,6},{5,7},{6,4},{7,5},{8,10},{9,11},{10,... | collective-permute-start | bytes 725000 | tf_op jit(solution)/shard_map/ppermute | solution.py:133
  36.9 3.5 %collective-permute-done.1.refs_3_ = bf16[944,128]{1,0:T(8,128)(2,1)S(1)} collective-permute-done((bf16[944,128]{1,0:T(8,128)(2,1)S(1)}, bf16[944,128]{1,0:T(8,128)(2,1)S(1)}, u32[]{:S(2)}, u32[]{:S(2)}) %collective-permute-start.1) | collective-permute-done | bytes 241696 | tf_op jit(solution)/shard_map/ppermute | solution.py:133
  40.4 1.3 %copy-done.1 = bf16[1,160,4096]{2,1,0:T(8,128)(2,1)S(1)} copy-done((bf16[1,160,4096]{2,1,0:T(8,128)(2,1)S(1)}, bf16[1,160,4096]{2,1,0:T(8,128)(2,1)}, u32[]{:S(2)}) %copy-start.1) | copy-done | bytes 1310744
  41.7 0.9 %copy-done.2 = bf16[944,128]{1,0:T(8,128)(2,1)S(1)} copy-done((bf16[944,128]{1,0:T(8,128)(2,1)S(1)}, bf16[944,128]{1,0:T(8,128)(2,1)}, u32[]{:S(2)}) %copy-start.2) | copy-done | bytes 241688
  42.7 0.9 %copy-done.3 = bf16[944,128]{1,0:T(8,128)(2,1)S(1)} copy-done((bf16[944,128]{1,0:T(8,128)(2,1)S(1)}, bf16[944,128]{1,0:T(8,128)(2,1)}, u32[]{:S(2)}) %copy-start.3) | copy-done | bytes 241688
  43.6 1.5 %shard_map.56 = (f32[160,128]{1,0:T(8,128)S(1)}, f32[160,128]{1,0:T(8,128)S(1)}) custom-call(bf16[160,11008]{1,0:T(8,128)(2,1)S(1)} %bitcast.4, bf16[160,4096]{1,0:T(8,128)(2,1)S(1)} %bitcast.6, bf16[944,128]{1,0:T(8,128)(2,1)S(1)} %copy-done.2, bf16[944,128]{1,0:T(8,128)(2,1)S(1)} %copy-done.3, bf16[944,128]{1,0:T(8,128)(2,1)S(1)} %collective-permute-done.refs_2_, ...), custom_call_target="tpu_custom_call" | custom-call | flops 309329920 | bytes 4349952 | tf_op jit(solution)/shard_map/pallas_call | solution.py:171
  45.2 0.4 collective-permute-done.9.refs_3_
  45.6 3.3 %collective-permute-done.7.refs_1_ = bf16[944,128]{1,0:T(8,128)(2,1)S(1)} collective-permute-done((bf16[944,128]{1,0:T(8,128)(2,1)S(1)}, bf16[944,128]{1,0:T(8,128)(2,1)S(1)}, u32[]{:S(2)}, u32[]{:S(2)}) %collective-permute-start.7) | collective-permute-done | bytes 241696 | tf_op jit(solution)/shard_map/ppermute | solution.py:133
  48.9 1.7 %shard_map.57 = (f32[32,80]{1,0:T(8,128)S(1)}, f32[32,80]{1,0:T(8,128)S(1)}) custom-call(bf16[160,11008]{1,0:T(8,128)(2,1)S(1)} %bitcast.5, bf16[160,4096]{1,0:T(8,128)(2,1)S(1)} %bitcast.7, f32[160,128]{1,0:T(8,128)S(1)} %get-tuple-element.13.in_ref, f32[160,128]{1,0:T(8,128)S(1)} %get-tuple-element.14.out_ref, ...), custom_call_target="tpu_custom_call" | custom-call | flops 309329920 | bytes 4349952 | tf_op jit(solution)/shard_map/pallas_call | solution.py:182
  50.6 0.0 collective-permute-start.14
  50.6 1.2 %collective-permute-done.14 = f32[32,80]{1,0:T(8,128)S(1)} collective-permute-done((f32[32,80]{1,0:T(8,128)S(1)}, f32[32,80]{1,0:T(8,128)S(1)}, u32[]{:S(2)}, u32[]{:S(2)}) %collective-permute-start.14) | collective-permute-done | bytes 10272 | tf_op jit(solution)/shard_map/ppermute | solution.py:133
  51.8 0.6 %add_bitcast_fusion = f32[80,32]{0,1:T(8,128)} fusion(f32[32,80]{1,0:T(8,128)S(1)} %get-tuple-element.15, f32[32,80]{1,0:T(8,128)S(1)} %collective-permute-done.14), kind=kLoop, calls=%fused_computation | loop fusion | flops 2560 | bytes 30720 | tf_op jit(solution)/shard_map/transpose | solution.py:191
  (10 shorter events, 0.0 us)
Async XLA Ops:
  0.0 40.4 %copy-start = (bf16[1,160,11008]{2,1,0:T(8,128)(2,1)S(1)}, bf16[1,160,11008]{2,1,0:T(8,128)(2,1)}, u32[]{:S(2)}) copy-start(bf16[1,160,11008]{2,1,0:T(8,128)(2,1)} %param.5) | copy-start | bytes 10567684
  3.0 15.5 %collective-permute-start.4 = (bf16[944,128]{1,0:T(8,128)(2,1)}, bf16[944,128]{1,0:T(8,128)(2,1)S(1)}, u32[]{:S(2)}, u32[]{:S(2)}) collective-permute-start(bf16[944,128]{1,0:T(8,128)(2,1)} %get-tuple-element.11.refs_0_), channel_id=1, source_target_pairs={{0,8},{1,9},{2,10},{3,11},{4,12},{5,13},{6,14},{7,15},{8,0},{9,1},... | collective-permute-start | bytes 725000 | tf_op jit(solution)/shard_map/ppermute | solution.py:133
  7.1 15.0 %collective-permute-start = (bf16[944,128]{1,0:T(8,128)(2,1)}, bf16[944,128]{1,0:T(8,128)(2,1)S(1)}, u32[]{:S(2)}, u32[]{:S(2)}) collective-permute-start(bf16[944,128]{1,0:T(8,128)(2,1)} %get-tuple-element.11.refs_0_), channel_id=1, source_target_pairs={{0,2},{1,3},{2,0},{3,1},{4,6},{5,7},{6,4},{7,5},{8,10},{9,11},{10,... | collective-permute-start | bytes 725000 | tf_op jit(solution)/shard_map/ppermute | solution.py:133
  8.5 15.0 %collective-permute-start.2 = (bf16[944,128]{1,0:T(8,128)(2,1)}, bf16[944,128]{1,0:T(8,128)(2,1)S(1)}, u32[]{:S(2)}, u32[]{:S(2)}) collective-permute-start(bf16[944,128]{1,0:T(8,128)(2,1)} %get-tuple-element.11.refs_0_), channel_id=1, source_target_pairs={{0,4},{1,5},{2,6},{3,7},{4,0},{5,1},{6,2},{7,3},{8,12},{9,13},{10,... | collective-permute-start | bytes 725000 | tf_op jit(solution)/shard_map/ppermute | solution.py:133
  18.4 8.8 %collective-permute-start.10 = (bf16[944,128]{1,0:T(8,128)(2,1)S(1)}, bf16[944,128]{1,0:T(8,128)(2,1)S(1)}, u32[]{:S(2)}, u32[]{:S(2)}) collective-permute-start(bf16[944,128]{1,0:T(8,128)(2,1)S(1)} %collective-permute-done.4.refs_6_), channel_id=1, source_target_pairs={{0,4},{1,5},{2,6},{3,7},{4,0},{5,1},{6,2},{7,3},{8,12},{9,13},{10,... | collective-permute-start | bytes 725000 | tf_op jit(solution)/shard_map/ppermute | solution.py:133
  19.2 11.4 %collective-permute-start.3 = (bf16[944,128]{1,0:T(8,128)(2,1)}, bf16[944,128]{1,0:T(8,128)(2,1)S(1)}, u32[]{:S(2)}, u32[]{:S(2)}) collective-permute-start(bf16[944,128]{1,0:T(8,128)(2,1)} %get-tuple-element.12.refs_1_), channel_id=1, source_target_pairs={{0,4},{1,5},{2,6},{3,7},{4,0},{5,1},{6,2},{7,3},{8,12},{9,13},{10,... | collective-permute-start | bytes 725000 | tf_op jit(solution)/shard_map/ppermute | solution.py:133
  20.4 11.5 %collective-permute-start.5 = (bf16[944,128]{1,0:T(8,128)(2,1)S(1)}, bf16[944,128]{1,0:T(8,128)(2,1)S(1)}, u32[]{:S(2)}, u32[]{:S(2)}) collective-permute-start(bf16[944,128]{1,0:T(8,128)(2,1)S(1)} %collective-permute-done.4.refs_6_), channel_id=1, source_target_pairs={{0,16},{1,17},{2,18},{3,19},{4,20},{5,21},{6,22},{7,23},{8,24},{9,... | collective-permute-start | bytes 725000 | tf_op jit(solution)/shard_map/ppermute | solution.py:133
  22.0 11.4 %collective-permute-start.8 = (bf16[944,128]{1,0:T(8,128)(2,1)S(1)}, bf16[944,128]{1,0:T(8,128)(2,1)S(1)}, u32[]{:S(2)}, u32[]{:S(2)}) collective-permute-start(bf16[944,128]{1,0:T(8,128)(2,1)S(1)} %collective-permute-done.4.refs_6_), channel_id=1, source_target_pairs={{0,2},{1,3},{2,0},{3,1},{4,6},{5,7},{6,4},{7,5},{8,10},{9,11},{10,... | collective-permute-start | bytes 725000 | tf_op jit(solution)/shard_map/ppermute | solution.py:133
  23.5 10.4 %collective-permute-start.6 = (bf16[944,128]{1,0:T(8,128)(2,1)S(1)}, bf16[944,128]{1,0:T(8,128)(2,1)S(1)}, u32[]{:S(2)}, u32[]{:S(2)}) collective-permute-start(bf16[944,128]{1,0:T(8,128)(2,1)S(1)} %collective-permute-done.2.refs_4_), channel_id=1, source_target_pairs={{0,2},{1,3},{2,0},{3,1},{4,6},{5,7},{6,4},{7,5},{8,10},{9,11},{10,... | collective-permute-start | bytes 725000 | tf_op jit(solution)/shard_map/ppermute | solution.py:133
  27.2 8.2 %collective-permute-start.11 = (bf16[944,128]{1,0:T(8,128)(2,1)S(1)}, bf16[944,128]{1,0:T(8,128)(2,1)S(1)}, u32[]{:S(2)}, u32[]{:S(2)}) collective-permute-start(bf16[944,128]{1,0:T(8,128)(2,1)S(1)} %collective-permute-done.10.refs_4_), channel_id=1, source_target_pairs={{0,16},{1,17},{2,18},{3,19},{4,20},{5,21},{6,22},{7,23},{8,24},{9,... | collective-permute-start | bytes 725000 | tf_op jit(solution)/shard_map/ppermute | solution.py:133
  30.6 9.8 %collective-permute-start.1 = (bf16[944,128]{1,0:T(8,128)(2,1)S(1)}, bf16[944,128]{1,0:T(8,128)(2,1)S(1)}, u32[]{:S(2)}, u32[]{:S(2)}) collective-permute-start(bf16[944,128]{1,0:T(8,128)(2,1)S(1)} %collective-permute-done.refs_2_), channel_id=1, source_target_pairs={{0,16},{1,17},{2,18},{3,19},{4,20},{5,21},{6,22},{7,23},{8,24},{9,... | collective-permute-start | bytes 725000 | tf_op jit(solution)/shard_map/ppermute | solution.py:133
  31.9 13.2 %collective-permute-start.12 = (bf16[944,128]{1,0:T(8,128)(2,1)S(1)}, bf16[944,128]{1,0:T(8,128)(2,1)S(1)}, u32[]{:S(2)}, u32[]{:S(2)}) collective-permute-start(bf16[944,128]{1,0:T(8,128)(2,1)S(1)} %collective-permute-done.10.refs_4_), channel_id=1, source_target_pairs={{0,2},{1,3},{2,0},{3,1},{4,6},{5,7},{6,4},{7,5},{8,10},{9,11},{10,... | collective-permute-start | bytes 725000 | tf_op jit(solution)/shard_map/ppermute | solution.py:133
  33.4 12.2 %collective-permute-start.9 = (bf16[944,128]{1,0:T(8,128)(2,1)S(1)}, bf16[944,128]{1,0:T(8,128)(2,1)S(1)}, u32[]{:S(2)}, u32[]{:S(2)}) collective-permute-start(bf16[944,128]{1,0:T(8,128)(2,1)S(1)} %collective-permute-done.8.refs_2_), channel_id=1, source_target_pairs={{0,16},{1,17},{2,18},{3,19},{4,20},{5,21},{6,22},{7,23},{8,24},{9,... | collective-permute-start | bytes 725000 | tf_op jit(solution)/shard_map/ppermute | solution.py:133
  33.9 15.0 %collective-permute-start.7 = (bf16[944,128]{1,0:T(8,128)(2,1)S(1)}, bf16[944,128]{1,0:T(8,128)(2,1)S(1)}, u32[]{:S(2)}, u32[]{:S(2)}) collective-permute-start(bf16[944,128]{1,0:T(8,128)(2,1)S(1)} %collective-permute-done.6.refs_0_), channel_id=1, source_target_pairs={{0,16},{1,17},{2,18},{3,19},{4,20},{5,21},{6,22},{7,23},{8,24},{9,... | collective-permute-start | bytes 725000 | tf_op jit(solution)/shard_map/ppermute | solution.py:133
  35.4 13.5 %collective-permute-start.13 = (bf16[944,128]{1,0:T(8,128)(2,1)S(1)}, bf16[944,128]{1,0:T(8,128)(2,1)S(1)}, u32[]{:S(2)}, u32[]{:S(2)}) collective-permute-start(bf16[944,128]{1,0:T(8,128)(2,1)S(1)} %collective-permute-done.11.refs_5_), channel_id=1, source_target_pairs={{0,2},{1,3},{2,0},{3,1},{4,6},{5,7},{6,4},{7,5},{8,10},{9,11},{10,... | collective-permute-start | bytes 725000 | tf_op jit(solution)/shard_map/ppermute | solution.py:133
  40.4 1.3 %copy-start.1 = (bf16[1,160,4096]{2,1,0:T(8,128)(2,1)S(1)}, bf16[1,160,4096]{2,1,0:T(8,128)(2,1)}, u32[]{:S(2)}) copy-start(bf16[1,160,4096]{2,1,0:T(8,128)(2,1)} %param.6) | copy-start | bytes 3932164
  41.7 0.9 %copy-start.2 = (bf16[944,128]{1,0:T(8,128)(2,1)S(1)}, bf16[944,128]{1,0:T(8,128)(2,1)}, u32[]{:S(2)}) copy-start(bf16[944,128]{1,0:T(8,128)(2,1)} %get-tuple-element.11.refs_0_) | copy-start | bytes 724996
  42.7 0.9 %copy-start.3 = (bf16[944,128]{1,0:T(8,128)(2,1)S(1)}, bf16[944,128]{1,0:T(8,128)(2,1)}, u32[]{:S(2)}) copy-start(bf16[944,128]{1,0:T(8,128)(2,1)} %get-tuple-element.12.refs_1_) | copy-start | bytes 724996
  50.6 1.2 %collective-permute-start.14 = (f32[32,80]{1,0:T(8,128)S(1)}, f32[32,80]{1,0:T(8,128)S(1)}, u32[]{:S(2)}, u32[]{:S(2)}) collective-permute-start(f32[32,80]{1,0:T(8,128)S(1)} %get-tuple-element.16), channel_id=1, source_target_pairs={{0,1},{1,0},{2,3},{3,2},{4,5},{5,4},{6,7},{7,6},{8,9},{9,8},{10,11... | collective-permute-start | bytes 30728 | tf_op jit(solution)/shard_map/ppermute | solution.py:133

commit v2 on v1

--- a/solution.py
+++ b/solution.py
@@ -34,24 +34,46 @@
     return lax.dynamic_slice_in_dim(summed, lax.axis_index("layer") * halves, halves, 0)
 
 
-def take_halves(half, ids_ref, in_ref, out_ref, own_ref, other_ref, sems):
-    chosen = ids_ref[lax.axis_index("layer")]
+MOVES = (
+    ((1, 0, 1), (0, 0, 1), 1, ()),
+    ((0, 1, 1), (0, 0, 1), "x", ()),
+    ((2, 0, 0), (0, 0, 0), 2, ()),
+    ((0, 1, 0), (0, 0, 0), "x", ()),
+    ((1, 1, 1), (1, 0, 1), "x", ()),
+    ((3, 0, 1), (1, 0, 1), 2, ()),
+    ((1, 0, 0), (1, 0, 1), "y", ((0, 1, 1),)),
+    ((2, 1, 0), (2, 0, 0), "x", ((1, 0, 1), (0, 1, 1),)),
+    ((3, 0, 0), (2, 0, 0), 1, ((1, 0, 1), (0, 1, 1), (0, 1, 0),)),
+    ((1, 1, 0), (1, 0, 0), "x", ((1, 0, 1), (0, 1, 1), (2, 0, 0), (0, 1, 0),)),
+    ((2, 0, 1), (2, 0, 0), "y", ((1, 0, 1), (0, 1, 1), (0, 1, 0), (1, 0, 0), (1, 1, 1),)),
+    ((3, 1, 0), (2, 1, 0), 1, ((1, 0, 1), (0, 1, 1), (2, 0, 0), (0, 1, 0), (1, 0, 0), (1, 1, 1),)),
+    ((2, 1, 1), (2, 1, 0), "y", ((1, 0, 1), (0, 1, 1), (2, 0, 0), (0, 1, 0), (1, 0, 0), (1, 1, 1), (3, 0, 1),)),
+    ((3, 1, 1), (3, 0, 1), "x", ((1, 0, 1), (0, 1, 1), (2, 0, 0), (0, 1, 0), (1, 0, 0), (1, 1, 1), (2, 1, 0), (3, 0, 0),)),
+)
+FIRST_SUM = ((0, 0), (0, 1), (1, 0), (3, 0))
+
+
+def take_halves(half, ids_ref, in_ref, out_ref, first_ref, second_ref, ids, sems):
+    fetch = pltpu.make_async_copy(ids_ref, ids, sems.at[3])
+    fetch.start()
+    fetch.wait()
+    chosen = ids[lax.axis_index("layer")]
     part = lax.axis_index("parts")
     tail = in_ref.shape[1] - half
 
-    def run(first_ref, second_ref):
+    def run(top_ref, bottom_ref):
         copies = (
-            pltpu.make_async_copy(in_ref.at[chosen, pl.ds(0, half)], first_ref, sems.at[0]),
-            pltpu.make_async_copy(in_ref.at[chosen, pl.ds(half, tail)], second_ref.at[pl.ds(0, tail)], sems.at[1]),
-            pltpu.make_async_copy(out_ref.at[chosen], second_ref.at[pl.ds(tail, half - tail)], sems.at[2]),
+            pltpu.make_async_copy(in_ref.at[chosen, pl.ds(0, half)], top_ref, sems.at[0]),
+            pltpu.make_async_copy(in_ref.at[chosen, pl.ds(half, tail)], bottom_ref.at[pl.ds(0, tail)], sems.at[1]),
+            pltpu.make_async_copy(out_ref.at[chosen], bottom_ref.at[pl.ds(tail, half - tail)], sems.at[2]),
         )
         for copy in copies:
             copy.start()
         for copy in copies:
             copy.wait()
 
-    pl.when(part == 0)(lambda: run(own_ref, other_ref))
-    pl.when(part == 1)(lambda: run(other_ref, own_ref))
+    pl.when(part == 0)(lambda: run(first_ref, second_ref))
+    pl.when(part == 1)(lambda: run(second_ref, first_ref))
 
 
 def add_blocks(offsets, in_rows, half, hidden_ref, grad_ref, pieces, window, acc_in, acc_out):
@@ -61,20 +83,20 @@
     tail = in_rows - half
     out_rows = half - tail
     for i, offset in enumerate(offsets):
-        own_ref, other_ref = pieces[2 * i], pieces[2 * i + 1]
+        first_ref, second_ref = pieces[2 * i], pieces[2 * i + 1]
         source = tok ^ offset
         row = source * in_rows
         start = jnp.minimum(row // LANES * LANES, hidden_ref.shape[1] - span)
         shift = pl.multiple_of(row - start, 32)
         window[i] = jnp.zeros((span, LANES), jnp.bfloat16)
 
-        def place(first_ref, second_ref):
-            window[i, pl.ds(shift, half), :] = first_ref[...]
-            window[i, pl.ds(pl.multiple_of(shift + half, 16), tail), :] = second_ref[:tail, :]
-
-        pl.when(part == 0)(lambda: place(own_ref, other_ref))
-        pl.when(part == 1)(lambda: place(other_ref, own_ref))
-        outward = jnp.where(part == 0, other_ref[tail:, :], own_ref[tail:, :])
+        def place(top_ref, bottom_ref):
+            window[i, pl.ds(shift, half), :] = top_ref[...]
+            window[i, pl.ds(pl.multiple_of(shift + half, 16), tail), :] = bottom_ref[:tail, :]
+
+        pl.when(part == 0)(lambda: place(first_ref, second_ref))
+        pl.when(part == 1)(lambda: place(second_ref, first_ref))
+        outward = jnp.where(part == 0, second_ref[tail:, :], first_ref[tail:, :])
         acc_in = acc_in + jnp.dot(
             hidden_ref[:, pl.ds(pl.multiple_of(start, LANES), span)], window[i], preferred_element_type=jnp.float32
         )
@@ -132,62 +154,45 @@
         ]
         return lax.ppermute(value, AXES, pairs)
 
-    across_x = functools.partial(swap, tok=1)
-    across_y = functools.partial(swap, part=1)
-    z_one = functools.partial(swap, tok=x_size)
-    z_two = functools.partial(swap, tok=2 * x_size)
-
+    partner = {"x": dict(tok=1), "y": dict(part=1), **{z: dict(tok=z * x_size) for z in (1, 2, 3)}}
     piece = jax.ShapeDtypeStruct((half, LANES), jnp.bfloat16)
-    own, other = pl.pallas_call(
+    in_hbm = [pltpu.with_memory_space_constraint(a, pltpu.HBM) for a in (layer_ids, factor_in, factor_out)]
+    have = dict(zip(((0, 0, 0), (0, 0, 1)), pl.pallas_call(
         functools.partial(take_halves, half),
         out_shape=(piece, piece),
-        in_specs=[pl.BlockSpec(memory_space=pltpu.SMEM)] + [pl.BlockSpec(memory_space=pl.ANY)] * 2,
+        in_specs=[pl.BlockSpec(memory_space=pl.ANY)] * 3,
         out_specs=[vmem] * 2,
-        scratch_shapes=[pltpu.SemaphoreType.DMA((3,))],
-    )(layer_ids, factor_in, factor_out)
-
-    z1, z2, x0 = z_one(own), z_two(own), across_x(own)
-    z1_other = z_one(other)
-    y0 = across_y(x0)
-    x1, x2, y2 = across_x(z1), across_x(z2), across_y(z2)
-    z3 = z_one(z2)
-    x3, y3 = across_x(z3), across_y(z3)
-    y1, y2x = across_y(x1), across_y(x2)
-    x3y = across_x(y3)
-
-    def cost(blocks):
-        return pl.CostEstimate(
-            flops=2 * rows * LANES * (in_rows + out_rows) * blocks,
-            bytes_accessed=2 * (rows + LANES) * (in_rows + out_rows) * blocks, transcendentals=0,
-        )
+        scratch_shapes=[pltpu.SMEM(layer_ids.shape, layer_ids.dtype), pltpu.SemaphoreType.DMA((4,))],
+        compiler_params=pltpu.CompilerParams(vmem_limit_bytes=4 << 20),
+    )(*in_hbm)))
+    for arrives, passed_on, across, waits in MOVES:
+        value = have[passed_on]
+        if waits:
+            value = lax.optimization_barrier((value, *(have[w] for w in waits)))[0]
+        have[arrives] = swap(value, **partner[across])
 
     span = -(-(in_rows + LANES) // LANES) * LANES
     total = jax.ShapeDtypeStruct((rows, LANES), jnp.float32)
-
-    def window(blocks):
-        return pltpu.VMEM((blocks, span, LANES), jnp.bfloat16)
-
-    near = (0, 1, x_size, 2 * x_size)
-    sums = pl.pallas_call(
-        functools.partial(early, near, in_rows, half),
-        out_shape=(total, total),
-        in_specs=[vmem] * 10,
-        out_specs=[vmem] * 2,
-        scratch_shapes=[window(4)],
-        cost_estimate=cost(4),
-        compiler_params=pltpu.CompilerParams(vmem_limit_bytes=24 << 20),
-    )(hidden, grad, own, other, x0, y0, z1, z1_other, z2, y2)
-    far = (x_size + 1, 2 * x_size + 1, 3 * x_size, 3 * x_size + 1)
-    score = jax.ShapeDtypeStruct((QUERIES, rows // 2), jnp.float32)
-    kept, sent = pl.pallas_call(
-        functools.partial(late, far, in_rows, half),
-        out_shape=(score, score),
-        in_specs=[vmem] * 12,
-        out_specs=[vmem] * 2,
-        scratch_shapes=[window(4)],
-        cost_estimate=cost(4),
-        compiler_params=pltpu.CompilerParams(vmem_limit_bytes=24 << 20),
-    )(hidden, grad, *sums, x1, y1, x2, y2x, z3, y3, x3, x3y)
+    score = jax.ShapeDtypeStruct((QUERIES, rows // layers), jnp.float32)
+
+    def products(kernel, blocks, result, *sums):
+        pieces = [have[z, x, side] for z, x in blocks for side in (0, 1)]
+        return pl.pallas_call(
+            functools.partial(kernel, [z * x_size + x for z, x in blocks], in_rows, half),
+            out_shape=(result, result),
+            in_specs=[vmem] * (2 + len(sums) + len(pieces)),
+            out_specs=[vmem] * 2,
+            scratch_shapes=[pltpu.VMEM((len(blocks), span, LANES), jnp.bfloat16)],
+            cost_estimate=pl.CostEstimate(
+                flops=2 * rows * LANES * (in_rows + out_rows) * len(blocks),
+                bytes_accessed=2 * (rows + LANES) * (in_rows + out_rows) * len(blocks), transcendentals=0,
+            ),
+            compiler_params=pltpu.CompilerParams(vmem_limit_bytes=24 << 20),
+        )(hidden, grad, *sums, *pieces)
+
+    last = [(z, x) for z in range(4) for x in range(2) if (z, x) not in FIRST_SUM]
+    sums = products(early, FIRST_SUM, total)
+    kept, sent = products(late, last, score, *sums)
     return (kept + swap(sent, layer=1)).T
 
 

time: 52.7 us -> 43.9 us (0.83)
  waiting for transfers between devices: 21.7 us -> 15.2 us
  local copies, waits for them, and re-layouts: 3.2 us -> 0.01 us
  starting transfers between devices: 20.7 us -> 22.3 us
  Pallas kernels: 6.18 us -> 5.54 us
    ppermute x15, waiting for transfers between devices: 21.7 us -> 15.2 us  [swap(): return lax.ppermute(value, AXES, pairs)]
    unnamed x8 -> x4, local copies, waits for them, and re-layouts: 3.2 us -> 0.01 us
    ppermute x15, starting transfers between devices: 20.7 us -> 22.3 us  [swap(): return lax.ppermute(value, AXES, pairs)]
    pallas_call x1, Pallas kernels: 2.94 us -> 2.31 us  [swapped_form(): pl.pallas_call(functools.partial(take_halves, half), out_shape=(piece, pi...]
  transfers between devices with their start and end apart: 15 -> 15, of which waited for: 7 -> 9; matrix products, arithmetic and copies ran while one was open for 0% -> 0% of each run, Pallas kernels for 3% -> 4%
where the time goes in v2:
time: 43.9 us; the launch traced here: 43.7 us
  starting transfers between devices  22.3 us (51%)
  waiting for transfers between devices  15.2 us (35%)
  Pallas kernels  5.54 us (13%)
  other arithmetic  0.61 us (1%)
    ppermute x15, starting transfers between devices, swap(): return lax.ppermute(value, AXES, pairs)  22.3 us
    ppermute x15, waiting for transfers between devices, swap(): return lax.ppermute(value, AXES, pairs)  15.2 us
    pallas_call x2, Pallas kernels, products(): pl.pallas_call(functools.partial(kernel, [z * x_size + x for z, x in bloc...  3.23 us
    pallas_call x1, Pallas kernels, swapped_form(): pl.pallas_call(functools.partial(take_halves, half), out_shape=(piece, pi...  2.31 us
  transfers between devices with their start and end apart: 15, of which 9 were waited for; matrix products, arithmetic and copies ran while one was open for 0% of the time, Pallas kernels for 4%

profile of v2, /device:TPU:0, one launch (start us, length us, event | category | flops | bytes accessed | tf_op | source)
XLA Modules:
  0.0 43.7 jit_solution(1282381608293349792)
XLA Ops:
  0.0 2.3 %shard_map.55 = (bf16[944,128]{1,0:T(8,128)(2,1)S(1)}, bf16[944,128]{1,0:T(8,128)(2,1)S(1)}) custom-call(s32[32]{0:T(128)} %ids_ref.1, bf16[32,1376,128]{2,1,0:T(8,128)(2,1)} %in_ref.1, bf16[32,512,128]{2,1,0:T(8,128)(2,1)} %out_ref.1), custom_call_target="tpu_custom_call" | custom-call | tf_op jit(solution)/shard_map/pallas_call | solution.py:160
  2.3 3.1 %collective-permute-start.2 = (bf16[944,128]{1,0:T(8,128)(2,1)S(1)}, bf16[944,128]{1,0:T(8,128)(2,1)S(1)}, u32[]{:S(2)}, u32[]{:S(2)}) collective-permute-start(bf16[944,128]{1,0:T(8,128)(2,1)S(1)} %get-tuple-element.20.refs_1_), channel_id=1, source_target_pairs={{0,4},{1,5},{2,6},{3,7},{4,0},{5,1},{6,2},{7,3},{8,12},{9,13},{10,... | collective-permute-start | bytes 725000 | tf_op jit(solution)/shard_map/ppermute | solution.py:155
  5.4 1.5 %collective-permute-start.1 = (bf16[944,128]{1,0:T(8,128)(2,1)S(1)}, bf16[944,128]{1,0:T(8,128)(2,1)S(1)}, u32[]{:S(2)}, u32[]{:S(2)}) collective-permute-start(bf16[944,128]{1,0:T(8,128)(2,1)S(1)} %get-tuple-element.20.refs_1_), channel_id=1, source_target_pairs={{0,2},{1,3},{2,0},{3,1},{4,6},{5,7},{6,4},{7,5},{8,10},{9,11},{10,... | collective-permute-start | bytes 725000 | tf_op jit(solution)/shard_map/ppermute | solution.py:155
  6.9 2.6 %collective-permute-start.4 = (bf16[944,128]{1,0:T(8,128)(2,1)S(1)}, bf16[944,128]{1,0:T(8,128)(2,1)S(1)}, u32[]{:S(2)}, u32[]{:S(2)}) collective-permute-start(bf16[944,128]{1,0:T(8,128)(2,1)S(1)} %get-tuple-element.19.refs_0_), channel_id=1, source_target_pairs={{0,8},{1,9},{2,10},{3,11},{4,12},{5,13},{6,14},{7,15},{8,0},{9,1},... | collective-permute-start | bytes 725000 | tf_op jit(solution)/shard_map/ppermute | solution.py:155
  9.5 0.5 %collective-permute-start = (bf16[944,128]{1,0:T(8,128)(2,1)S(1)}, bf16[944,128]{1,0:T(8,128)(2,1)S(1)}, u32[]{:S(2)}, u32[]{:S(2)}) collective-permute-start(bf16[944,128]{1,0:T(8,128)(2,1)S(1)} %get-tuple-element.19.refs_0_), channel_id=1, source_target_pairs={{0,2},{1,3},{2,0},{3,1},{4,6},{5,7},{6,4},{7,5},{8,10},{9,11},{10,... | collective-permute-start | bytes 725000 | tf_op jit(solution)/shard_map/ppermute | solution.py:155
  10.0 5.1 %collective-permute-done.2.refs_5_ = bf16[944,128]{1,0:T(8,128)(2,1)S(1)} collective-permute-done((bf16[944,128]{1,0:T(8,128)(2,1)S(1)}, bf16[944,128]{1,0:T(8,128)(2,1)S(1)}, u32[]{:S(2)}, u32[]{:S(2)}) %collective-permute-start.2) | collective-permute-done | bytes 241696 | tf_op jit(solution)/shard_map/ppermute | solution.py:155
  15.1 0.0 collective-permute-done.1.refs_3_
  15.1 2.6 %collective-permute-start.8 = (bf16[944,128]{1,0:T(8,128)(2,1)S(1)}, bf16[944,128]{1,0:T(8,128)(2,1)S(1)}, u32[]{:S(2)}, u32[]{:S(2)}) collective-permute-start(bf16[944,128]{1,0:T(8,128)(2,1)S(1)} %collective-permute-done.2.refs_5_), channel_id=1, source_target_pairs={{0,2},{1,3},{2,0},{3,1},{4,6},{5,7},{6,4},{7,5},{8,10},{9,11},{10,... | collective-permute-start | bytes 725000 | tf_op jit(solution)/shard_map/ppermute | solution.py:155
  17.7 1.5 %collective-permute-start.3 = (bf16[944,128]{1,0:T(8,128)(2,1)S(1)}, bf16[944,128]{1,0:T(8,128)(2,1)S(1)}, u32[]{:S(2)}, u32[]{:S(2)}) collective-permute-start(bf16[944,128]{1,0:T(8,128)(2,1)S(1)} %collective-permute-done.2.refs_5_), channel_id=1, source_target_pairs={{0,16},{1,17},{2,18},{3,19},{4,20},{5,21},{6,22},{7,23},{8,24},{9,... | collective-permute-start | bytes 725000 | tf_op jit(solution)/shard_map/ppermute | solution.py:155
  19.3 0.8 %collective-permute-done.4.refs_2_ = bf16[944,128]{1,0:T(8,128)(2,1)S(1)} collective-permute-done((bf16[944,128]{1,0:T(8,128)(2,1)S(1)}, bf16[944,128]{1,0:T(8,128)(2,1)S(1)}, u32[]{:S(2)}, u32[]{:S(2)}) %collective-permute-start.4) | collective-permute-done | bytes 241696 | tf_op jit(solution)/shard_map/ppermute | solution.py:155
  20.1 0.5 %collective-permute-start.10 = (bf16[944,128]{1,0:T(8,128)(2,1)S(1)}, bf16[944,128]{1,0:T(8,128)(2,1)S(1)}, u32[]{:S(2)}, u32[]{:S(2)}) collective-permute-start(bf16[944,128]{1,0:T(8,128)(2,1)S(1)} %collective-permute-done.4.refs_2_), channel_id=1, source_target_pairs={{0,2},{1,3},{2,0},{3,1},{4,6},{5,7},{6,4},{7,5},{8,10},{9,11},{10,... | collective-permute-start | bytes 725000 | tf_op jit(solution)/shard_map/ppermute | solution.py:155
  20.6 0.1 collective-permute-start.6
  20.7 0.0 collective-permute-done.refs_2_
  20.7 3.0 %collective-permute-start.5 = (bf16[944,128]{1,0:T(8,128)(2,1)S(1)}, bf16[944,128]{1,0:T(8,128)(2,1)S(1)}, u32[]{:S(2)}, u32[]{:S(2)}) collective-permute-start(bf16[944,128]{1,0:T(8,128)(2,1)S(1)} %collective-permute-done.4.refs_2_), channel_id=1, source_target_pairs={{0,4},{1,5},{2,6},{3,7},{4,0},{5,1},{6,2},{7,3},{8,12},{9,13},{10,... | collective-permute-start | bytes 725000 | tf_op jit(solution)/shard_map/ppermute | solution.py:155
  23.6 0.9 %collective-permute-done.8.refs_1_ = bf16[944,128]{1,0:T(8,128)(2,1)S(1)} collective-permute-done((bf16[944,128]{1,0:T(8,128)(2,1)S(1)}, bf16[944,128]{1,0:T(8,128)(2,1)S(1)}, u32[]{:S(2)}, u32[]{:S(2)}) %collective-permute-start.8) | collective-permute-done | bytes 241696 | tf_op jit(solution)/shard_map/ppermute | solution.py:155
  24.5 2.0 %collective-permute-start.7 = (bf16[944,128]{1,0:T(8,128)(2,1)S(1)}, bf16[944,128]{1,0:T(8,128)(2,1)S(1)}, u32[]{:S(2)}, u32[]{:S(2)}) collective-permute-start(bf16[944,128]{1,0:T(8,128)(2,1)S(1)} %collective-permute-done.3.refs_4_), channel_id=1, source_target_pairs={{0,2},{1,3},{2,0},{3,1},{4,6},{5,7},{6,4},{7,5},{8,10},{9,11},{10,... | collective-permute-start | bytes 725000 | tf_op jit(solution)/shard_map/ppermute | solution.py:155
  26.6 1.5 %collective-permute-start.9 = (bf16[944,128]{1,0:T(8,128)(2,1)S(1)}, bf16[944,128]{1,0:T(8,128)(2,1)S(1)}, u32[]{:S(2)}, u32[]{:S(2)}) collective-permute-start(bf16[944,128]{1,0:T(8,128)(2,1)S(1)} %collective-permute-done.4.refs_2_), channel_id=1, source_target_pairs={{0,16},{1,17},{2,18},{3,19},{4,20},{5,21},{6,22},{7,23},{8,24},{9,... | collective-permute-start | bytes 725000 | tf_op jit(solution)/shard_map/ppermute | solution.py:155
  28.1 1.6 %collective-permute-done.10.refs_4_ = bf16[944,128]{1,0:T(8,128)(2,1)S(1)} collective-permute-done((bf16[944,128]{1,0:T(8,128)(2,1)S(1)}, bf16[944,128]{1,0:T(8,128)(2,1)S(1)}, u32[]{:S(2)}, u32[]{:S(2)}) %collective-permute-start.10) | collective-permute-done | bytes 241696 | tf_op jit(solution)/shard_map/ppermute | solution.py:155
  29.7 1.9 %collective-permute-done.6.refs_7_ = bf16[944,128]{1,0:T(8,128)(2,1)S(1)} collective-permute-done((bf16[944,128]{1,0:T(8,128)(2,1)S(1)}, bf16[944,128]{1,0:T(8,128)(2,1)S(1)}, u32[]{:S(2)}, u32[]{:S(2)}) %collective-permute-start.6) | collective-permute-done | bytes 241696 | tf_op jit(solution)/shard_map/ppermute | solution.py:155
  31.6 0.0 collective-permute-done.5.refs_6_
  31.7 1.9 %collective-permute-start.13 = (bf16[944,128]{1,0:T(8,128)(2,1)S(1)}, bf16[944,128]{1,0:T(8,128)(2,1)S(1)}, u32[]{:S(2)}, u32[]{:S(2)}) collective-permute-start(bf16[944,128]{1,0:T(8,128)(2,1)S(1)} %collective-permute-done.6.refs_7_), channel_id=1, source_target_pairs={{0,2},{1,3},{2,0},{3,1},{4,6},{5,7},{6,4},{7,5},{8,10},{9,11},{10,... | collective-permute-start | bytes 725000 | tf_op jit(solution)/shard_map/ppermute | solution.py:155
  33.5 0.5 %collective-permute-start.11 = (bf16[944,128]{1,0:T(8,128)(2,1)S(1)}, bf16[944,128]{1,0:T(8,128)(2,1)S(1)}, u32[]{:S(2)}, u32[]{:S(2)}) collective-permute-start(bf16[944,128]{1,0:T(8,128)(2,1)S(1)} %collective-permute-done.10.refs_4_), channel_id=1, source_target_pairs={{0,16},{1,17},{2,18},{3,19},{4,20},{5,21},{6,22},{7,23},{8,24},{9,... | collective-permute-start | bytes 725000 | tf_op jit(solution)/shard_map/ppermute | solution.py:155
  34.0 0.9 %collective-permute-start.12 = (bf16[944,128]{1,0:T(8,128)(2,1)S(1)}, bf16[944,128]{1,0:T(8,128)(2,1)S(1)}, u32[]{:S(2)}, u32[]{:S(2)}) collective-permute-start(bf16[944,128]{1,0:T(8,128)(2,1)S(1)} %collective-permute-done.10.refs_4_), channel_id=1, source_target_pairs={{0,4},{1,5},{2,6},{3,7},{4,0},{5,1},{6,2},{7,3},{8,12},{9,13},{10,... | collective-permute-start | bytes 725000 | tf_op jit(solution)/shard_map/ppermute | solution.py:155
  35.0 1.5 %shard_map.56 = (f32[160,128]{1,0:T(8,128)S(1)}, f32[160,128]{1,0:T(8,128)S(1)}) custom-call(bf16[160,11008]{1,0:T(8,128)(2,1)S(1)} %bitcast.4, bf16[160,4096]{1,0:T(8,128)(2,1)S(1)} %bitcast.6, bf16[944,128]{1,0:T(8,128)(2,1)S(1)} %get-tuple-element.19.refs_0_, bf16[944,128]{1,0:T(8,128)(2,1)S(1)} %get-tuple-element.20.refs_1_, ...), custom_call_target="tpu_custom_call" | custom-call | flops 309329920 | bytes 4349952 | tf_op jit(solution)/shard_map/pallas_call | solution.py:180
  36.5 0.0 collective-permute-done.9.refs_3_
  36.5 2.1 %collective-permute-done.13.refs_7_ = bf16[944,128]{1,0:T(8,128)(2,1)S(1)} collective-permute-done((bf16[944,128]{1,0:T(8,128)(2,1)S(1)}, bf16[944,128]{1,0:T(8,128)(2,1)S(1)}, u32[]{:S(2)}, u32[]{:S(2)}) %collective-permute-start.13) | collective-permute-done | bytes 241696 | tf_op jit(solution)/shard_map/ppermute | solution.py:155
  38.6 1.4 %collective-permute-done.11.refs_5_ = bf16[944,128]{1,0:T(8,128)(2,1)S(1)} collective-permute-done((bf16[944,128]{1,0:T(8,128)(2,1)S(1)}, bf16[944,128]{1,0:T(8,128)(2,1)S(1)}, u32[]{:S(2)}, u32[]{:S(2)}) %collective-permute-start.11) | collective-permute-done | bytes 241696 | tf_op jit(solution)/shard_map/ppermute | solution.py:155
  40.0 0.2 collective-permute-done.12.refs_6_
  40.2 1.7 %shard_map.57 = (f32[32,80]{1,0:T(8,128)S(1)}, f32[32,80]{1,0:T(8,128)S(1)}) custom-call(bf16[160,11008]{1,0:T(8,128)(2,1)S(1)} %bitcast.5, bf16[160,4096]{1,0:T(8,128)(2,1)S(1)} %bitcast.7, f32[160,128]{1,0:T(8,128)S(1)} %get-tuple-element.23.in_ref, f32[160,128]{1,0:T(8,128)S(1)} %get-tuple-element.24.out_ref, ...), custom_call_target="tpu_custom_call" | custom-call | flops 309329920 | bytes 4349952 | tf_op jit(solution)/shard_map/pallas_call | solution.py:180
  41.9 0.0 collective-permute-start.14
  41.9 1.2 %collective-permute-done.14 = f32[32,80]{1,0:T(8,128)S(1)} collective-permute-done((f32[32,80]{1,0:T(8,128)S(1)}, f32[32,80]{1,0:T(8,128)S(1)}, u32[]{:S(2)}, u32[]{:S(2)}) %collective-permute-start.14) | collective-permute-done | bytes 10272 | tf_op jit(solution)/shard_map/ppermute | solution.py:155
  43.1 0.6 %add_bitcast_fusion = f32[80,32]{0,1:T(8,128)} fusion(f32[32,80]{1,0:T(8,128)S(1)} %get-tuple-element.31, f32[32,80]{1,0:T(8,128)S(1)} %collective-permute-done.14), kind=kLoop, calls=%fused_computation | loop fusion | flops 2560 | bytes 30720 | tf_op jit(solution)/shard_map/transpose | solution.py:196
  (6 shorter events, 0.0 us)
Async XLA Ops:
  0.0 35.0 %copy-start.1 = (bf16[1,160,4096]{2,1,0:T(8,128)(2,1)S(1)}, bf16[1,160,4096]{2,1,0:T(8,128)(2,1)}, u32[]{:S(2)}) copy-start(bf16[1,160,4096]{2,1,0:T(8,128)(2,1)} %param.6) | copy-start | bytes 3932164
  0.0 35.0 %copy-start = (bf16[1,160,11008]{2,1,0:T(8,128)(2,1)S(1)}, bf16[1,160,11008]{2,1,0:T(8,128)(2,1)}, u32[]{:S(2)}) copy-start(bf16[1,160,11008]{2,1,0:T(8,128)(2,1)} %param.5) | copy-start | bytes 10567684
  2.3 12.8 %collective-permute-start.2 = (bf16[944,128]{1,0:T(8,128)(2,1)S(1)}, bf16[944,128]{1,0:T(8,128)(2,1)S(1)}, u32[]{:S(2)}, u32[]{:S(2)}) collective-permute-start(bf16[944,128]{1,0:T(8,128)(2,1)S(1)} %get-tuple-element.20.refs_1_), channel_id=1, source_target_pairs={{0,4},{1,5},{2,6},{3,7},{4,0},{5,1},{6,2},{7,3},{8,12},{9,13},{10,... | collective-permute-start | bytes 725000 | tf_op jit(solution)/shard_map/ppermute | solution.py:155
  5.4 9.7 %collective-permute-start.1 = (bf16[944,128]{1,0:T(8,128)(2,1)S(1)}, bf16[944,128]{1,0:T(8,128)(2,1)S(1)}, u32[]{:S(2)}, u32[]{:S(2)}) collective-permute-start(bf16[944,128]{1,0:T(8,128)(2,1)S(1)} %get-tuple-element.20.refs_1_), channel_id=1, source_target_pairs={{0,2},{1,3},{2,0},{3,1},{4,6},{5,7},{6,4},{7,5},{8,10},{9,11},{10,... | collective-permute-start | bytes 725000 | tf_op jit(solution)/shard_map/ppermute | solution.py:155
  6.9 13.2 %collective-permute-start.4 = (bf16[944,128]{1,0:T(8,128)(2,1)S(1)}, bf16[944,128]{1,0:T(8,128)(2,1)S(1)}, u32[]{:S(2)}, u32[]{:S(2)}) collective-permute-start(bf16[944,128]{1,0:T(8,128)(2,1)S(1)} %get-tuple-element.19.refs_0_), channel_id=1, source_target_pairs={{0,8},{1,9},{2,10},{3,11},{4,12},{5,13},{6,14},{7,15},{8,0},{9,1},... | collective-permute-start | bytes 725000 | tf_op jit(solution)/shard_map/ppermute | solution.py:155
  9.5 11.2 %collective-permute-start = (bf16[944,128]{1,0:T(8,128)(2,1)S(1)}, bf16[944,128]{1,0:T(8,128)(2,1)S(1)}, u32[]{:S(2)}, u32[]{:S(2)}) collective-permute-start(bf16[944,128]{1,0:T(8,128)(2,1)S(1)} %get-tuple-element.19.refs_0_), channel_id=1, source_target_pairs={{0,2},{1,3},{2,0},{3,1},{4,6},{5,7},{6,4},{7,5},{8,10},{9,11},{10,... | collective-permute-start | bytes 725000 | tf_op jit(solution)/shard_map/ppermute | solution.py:155
  15.1 9.4 %collective-permute-start.8 = (bf16[944,128]{1,0:T(8,128)(2,1)S(1)}, bf16[944,128]{1,0:T(8,128)(2,1)S(1)}, u32[]{:S(2)}, u32[]{:S(2)}) collective-permute-start(bf16[944,128]{1,0:T(8,128)(2,1)S(1)} %collective-permute-done.2.refs_5_), channel_id=1, source_target_pairs={{0,2},{1,3},{2,0},{3,1},{4,6},{5,7},{6,4},{7,5},{8,10},{9,11},{10,... | collective-permute-start | bytes 725000 | tf_op jit(solution)/shard_map/ppermute | solution.py:155
  17.7 6.8 %collective-permute-start.3 = (bf16[944,128]{1,0:T(8,128)(2,1)S(1)}, bf16[944,128]{1,0:T(8,128)(2,1)S(1)}, u32[]{:S(2)}, u32[]{:S(2)}) collective-permute-start(bf16[944,128]{1,0:T(8,128)(2,1)S(1)} %collective-permute-done.2.refs_5_), channel_id=1, source_target_pairs={{0,16},{1,17},{2,18},{3,19},{4,20},{5,21},{6,22},{7,23},{8,24},{9,... | collective-permute-start | bytes 725000 | tf_op jit(solution)/shard_map/ppermute | solution.py:155
  20.1 9.6 %collective-permute-start.10 = (bf16[944,128]{1,0:T(8,128)(2,1)S(1)}, bf16[944,128]{1,0:T(8,128)(2,1)S(1)}, u32[]{:S(2)}, u32[]{:S(2)}) collective-permute-start(bf16[944,128]{1,0:T(8,128)(2,1)S(1)} %collective-permute-done.4.refs_2_), channel_id=1, source_target_pairs={{0,2},{1,3},{2,0},{3,1},{4,6},{5,7},{6,4},{7,5},{8,10},{9,11},{10,... | collective-permute-start | bytes 725000 | tf_op jit(solution)/shard_map/ppermute | solution.py:155
  20.6 11.0 %collective-permute-start.6 = (bf16[944,128]{1,0:T(8,128)(2,1)S(1)}, bf16[944,128]{1,0:T(8,128)(2,1)S(1)}, u32[]{:S(2)}, u32[]{:S(2)}) collective-permute-start(bf16[944,128]{1,0:T(8,128)(2,1)S(1)} %collective-permute-done.2.refs_5_), channel_id=1, source_target_pairs={{0,8},{1,9},{2,10},{3,11},{4,12},{5,13},{6,14},{7,15},{8,0},{9,1},... | collective-permute-start | bytes 725000 | tf_op jit(solution)/shard_map/ppermute | solution.py:155
  20.7 11.0 %collective-permute-start.5 = (bf16[944,128]{1,0:T(8,128)(2,1)S(1)}, bf16[944,128]{1,0:T(8,128)(2,1)S(1)}, u32[]{:S(2)}, u32[]{:S(2)}) collective-permute-start(bf16[944,128]{1,0:T(8,128)(2,1)S(1)} %collective-permute-done.4.refs_2_), channel_id=1, source_target_pairs={{0,4},{1,5},{2,6},{3,7},{4,0},{5,1},{6,2},{7,3},{8,12},{9,13},{10,... | collective-permute-start | bytes 725000 | tf_op jit(solution)/shard_map/ppermute | solution.py:155
  24.5 12.0 %collective-permute-start.7 = (bf16[944,128]{1,0:T(8,128)(2,1)S(1)}, bf16[944,128]{1,0:T(8,128)(2,1)S(1)}, u32[]{:S(2)}, u32[]{:S(2)}) collective-permute-start(bf16[944,128]{1,0:T(8,128)(2,1)S(1)} %collective-permute-done.3.refs_4_), channel_id=1, source_target_pairs={{0,2},{1,3},{2,0},{3,1},{4,6},{5,7},{6,4},{7,5},{8,10},{9,11},{10,... | collective-permute-start | bytes 725000 | tf_op jit(solution)/shard_map/ppermute | solution.py:155
  26.6 10.0 %collective-permute-start.9 = (bf16[944,128]{1,0:T(8,128)(2,1)S(1)}, bf16[944,128]{1,0:T(8,128)(2,1)S(1)}, u32[]{:S(2)}, u32[]{:S(2)}) collective-permute-start(bf16[944,128]{1,0:T(8,128)(2,1)S(1)} %collective-permute-done.4.refs_2_), channel_id=1, source_target_pairs={{0,16},{1,17},{2,18},{3,19},{4,20},{5,21},{6,22},{7,23},{8,24},{9,... | collective-permute-start | bytes 725000 | tf_op jit(solution)/shard_map/ppermute | solution.py:155
  31.7 6.9 %collective-permute-start.13 = (bf16[944,128]{1,0:T(8,128)(2,1)S(1)}, bf16[944,128]{1,0:T(8,128)(2,1)S(1)}, u32[]{:S(2)}, u32[]{:S(2)}) collective-permute-start(bf16[944,128]{1,0:T(8,128)(2,1)S(1)} %collective-permute-done.6.refs_7_), channel_id=1, source_target_pairs={{0,2},{1,3},{2,0},{3,1},{4,6},{5,7},{6,4},{7,5},{8,10},{9,11},{10,... | collective-permute-start | bytes 725000 | tf_op jit(solution)/shard_map/ppermute | solution.py:155
  33.5 6.5 %collective-permute-start.11 = (bf16[944,128]{1,0:T(8,128)(2,1)S(1)}, bf16[944,128]{1,0:T(8,128)(2,1)S(1)}, u32[]{:S(2)}, u32[]{:S(2)}) collective-permute-start(bf16[944,128]{1,0:T(8,128)(2,1)S(1)} %collective-permute-done.10.refs_4_), channel_id=1, source_target_pairs={{0,16},{1,17},{2,18},{3,19},{4,20},{5,21},{6,22},{7,23},{8,24},{9,... | collective-permute-start | bytes 725000 | tf_op jit(solution)/shard_map/ppermute | solution.py:155
  34.0 6.2 %collective-permute-start.12 = (bf16[944,128]{1,0:T(8,128)(2,1)S(1)}, bf16[944,128]{1,0:T(8,128)(2,1)S(1)}, u32[]{:S(2)}, u32[]{:S(2)}) collective-permute-start(bf16[944,128]{1,0:T(8,128)(2,1)S(1)} %collective-permute-done.10.refs_4_), channel_id=1, source_target_pairs={{0,4},{1,5},{2,6},{3,7},{4,0},{5,1},{6,2},{7,3},{8,12},{9,13},{10,... | collective-permute-start | bytes 725000 | tf_op jit(solution)/shard_map/ppermute | solution.py:155
  41.9 1.2 %collective-permute-start.14 = (f32[32,80]{1,0:T(8,128)S(1)}, f32[32,80]{1,0:T(8,128)S(1)}, u32[]{:S(2)}, u32[]{:S(2)}) collective-permute-start(f32[32,80]{1,0:T(8,128)S(1)} %get-tuple-element.32), channel_id=1, source_target_pairs={{0,1},{1,0},{2,3},{3,2},{4,5},{5,4},{6,7},{7,6},{8,9},{9,8},{10,11... | collective-permute-start | bytes 30728 | tf_op jit(solution)/shard_map/ppermute | solution.py:155

commit v3 on v2

--- a/solution.py
+++ b/solution.py
@@ -37,8 +37,8 @@
 MOVES = (
     ((1, 0, 1), (0, 0, 1), 1, ()),
     ((0, 1, 1), (0, 0, 1), "x", ()),
+    ((0, 1, 0), (0, 0, 0), "x", ()),
     ((2, 0, 0), (0, 0, 0), 2, ()),
-    ((0, 1, 0), (0, 0, 0), "x", ()),
     ((1, 1, 1), (1, 0, 1), "x", ()),
     ((3, 0, 1), (1, 0, 1), 2, ()),
     ((1, 0, 0), (1, 0, 1), "y", ((0, 1, 1),)),
@@ -47,10 +47,14 @@
     ((1, 1, 0), (1, 0, 0), "x", ((1, 0, 1), (0, 1, 1), (2, 0, 0), (0, 1, 0),)),
     ((2, 0, 1), (2, 0, 0), "y", ((1, 0, 1), (0, 1, 1), (0, 1, 0), (1, 0, 0), (1, 1, 1),)),
     ((3, 1, 0), (2, 1, 0), 1, ((1, 0, 1), (0, 1, 1), (2, 0, 0), (0, 1, 0), (1, 0, 0), (1, 1, 1),)),
-    ((2, 1, 1), (2, 1, 0), "y", ((1, 0, 1), (0, 1, 1), (2, 0, 0), (0, 1, 0), (1, 0, 0), (1, 1, 1), (3, 0, 1),)),
-    ((3, 1, 1), (3, 0, 1), "x", ((1, 0, 1), (0, 1, 1), (2, 0, 0), (0, 1, 0), (1, 0, 0), (1, 1, 1), (2, 1, 0), (3, 0, 0),)),
+    ((3, 1, 1), (3, 0, 1), "x", ((1, 0, 1), (0, 1, 1), (2, 0, 0), (0, 1, 0), (1, 0, 0), (1, 1, 1), (2, 1, 0),)),
+    ((2, 1, 1), (2, 1, 0), "y", ((1, 0, 1), (0, 1, 1), (2, 0, 0), (0, 1, 0), (1, 0, 0), (1, 1, 1), (3, 0, 1), (3, 0, 0),)),
 )
-FIRST_SUM = ((0, 0), (0, 1), (1, 0), (3, 0))
+SUMS = (
+    ((0, 0), (0, 1), (1, 0), (1, 1), (2, 0), (3, 0)),
+    ((3, 1),),
+    ((2, 1),),
+)
 
 
 def take_halves(half, ids_ref, in_ref, out_ref, first_ref, second_ref, ids, sems):
@@ -112,6 +116,13 @@
     zero = jnp.zeros(in_ref.shape, jnp.float32)
     in_ref[...], out_ref[...] = add_blocks(
         offsets, in_rows, half, hidden_ref, grad_ref, pieces, window, zero, zero
+    )
+
+
+def middle(offsets, in_rows, half, hidden_ref, grad_ref, in_before, out_before, *refs):
+    pieces, (in_ref, out_ref, window) = refs[:-3], refs[-3:]
+    in_ref[...], out_ref[...] = add_blocks(
+        offsets, in_rows, half, hidden_ref, grad_ref, pieces, window, in_before[...], out_before[...]
     )
 
 
@@ -190,9 +201,10 @@
             compiler_params=pltpu.CompilerParams(vmem_limit_bytes=24 << 20),
         )(hidden, grad, *sums, *pieces)
 
-    last = [(z, x) for z in range(4) for x in range(2) if (z, x) not in FIRST_SUM]
-    sums = products(early, FIRST_SUM, total)
-    kept, sent = products(late, last, score, *sums)
+    sums = products(early, SUMS[0], total)
+    for blocks in SUMS[1:-1]:
+        sums = products(middle, blocks, total, *sums)
+    kept, sent = products(late, SUMS[-1], score, *sums)
     return (kept + swap(sent, layer=1)).T
 
 

time: 43.9 us -> 41.7 us (0.950)
  waiting for transfers between devices: 15.2 us -> 13.8 us
  starting transfers between devices: 22.3 us -> 21.4 us
    ppermute x15, waiting for transfers between devices: 15.2 us -> 13.8 us  [swap(): return lax.ppermute(value, AXES, pairs)]
    ppermute x15, starting transfers between devices: 22.3 us -> 21.4 us  [swap(): return lax.ppermute(value, AXES, pairs)]
    pallas_call x2 -> x3, Pallas kernels: 3.23 us -> 3.32 us  [products(): pl.pallas_call(functools.partial(kernel, [z * x_size + x for z, x in bloc...]
  transfers between devices with their start and end apart: 15 -> 15, of which waited for: 9 -> 6; matrix products, arithmetic and copies ran while one was open for 0% -> 0% of each run, Pallas kernels for 4% -> 7%
where the time goes in v3:
time: 41.7 us; the launch traced here: 41.5 us
  starting transfers between devices  21.4 us (51%)
  waiting for transfers between devices  13.8 us (33%)
  Pallas kernels  5.63 us (14%)
  other arithmetic  0.61 us (1%)
    ppermute x15, starting transfers between devices, swap(): return lax.ppermute(value, AXES, pairs)  21.4 us
    ppermute x15, waiting for transfers between devices, swap(): return lax.ppermute(value, AXES, pairs)  13.8 us
    pallas_call x3, Pallas kernels, products(): pl.pallas_call(functools.partial(kernel, [z * x_size + x for z, x in bloc...  3.32 us
    pallas_call x1, Pallas kernels, swapped_form(): pl.pallas_call(functools.partial(take_halves, half), out_shape=(piece, pi...  2.31 us
  transfers between devices with their start and end apart: 15, of which 6 were waited for; matrix products, arithmetic and copies ran while one was open for 0% of the time, Pallas kernels for 7%

profile of v3, /device:TPU:0, one launch (start us, length us, event | category | flops | bytes accessed | tf_op | source)
XLA Modules:
  0.0 41.5 jit_solution(9295167196767464290)
XLA Ops:
  0.0 2.3 %shard_map.55 = (bf16[944,128]{1,0:T(8,128)(2,1)S(1)}, bf16[944,128]{1,0:T(8,128)(2,1)S(1)}) custom-call(s32[32]{0:T(128)} %ids_ref.1, bf16[32,1376,128]{2,1,0:T(8,128)(2,1)} %in_ref.1, bf16[32,512,128]{2,1,0:T(8,128)(2,1)} %out_ref.1), custom_call_target="tpu_custom_call" | custom-call | tf_op jit(solution)/shard_map/pallas_call | solution.py:171
  2.3 3.1 %collective-permute-start.2 = (bf16[944,128]{1,0:T(8,128)(2,1)S(1)}, bf16[944,128]{1,0:T(8,128)(2,1)S(1)}, u32[]{:S(2)}, u32[]{:S(2)}) collective-permute-start(bf16[944,128]{1,0:T(8,128)(2,1)S(1)} %get-tuple-element.22.refs_1_), channel_id=1, source_target_pairs={{0,4},{1,5},{2,6},{3,7},{4,0},{5,1},{6,2},{7,3},{8,12},{9,13},{10,... | collective-permute-start | bytes 725000 | tf_op jit(solution)/shard_map/ppermute | solution.py:166
  5.4 1.5 %collective-permute-start.1 = (bf16[944,128]{1,0:T(8,128)(2,1)S(1)}, bf16[944,128]{1,0:T(8,128)(2,1)S(1)}, u32[]{:S(2)}, u32[]{:S(2)}) collective-permute-start(bf16[944,128]{1,0:T(8,128)(2,1)S(1)} %get-tuple-element.22.refs_1_), channel_id=1, source_target_pairs={{0,2},{1,3},{2,0},{3,1},{4,6},{5,7},{6,4},{7,5},{8,10},{9,11},{10,... | collective-permute-start | bytes 725000 | tf_op jit(solution)/shard_map/ppermute | solution.py:166
  6.9 2.6 %collective-permute-start.4 = (bf16[944,128]{1,0:T(8,128)(2,1)S(1)}, bf16[944,128]{1,0:T(8,128)(2,1)S(1)}, u32[]{:S(2)}, u32[]{:S(2)}) collective-permute-start(bf16[944,128]{1,0:T(8,128)(2,1)S(1)} %get-tuple-element.21.refs_0_), channel_id=1, source_target_pairs={{0,8},{1,9},{2,10},{3,11},{4,12},{5,13},{6,14},{7,15},{8,0},{9,1},... | collective-permute-start | bytes 725000 | tf_op jit(solution)/shard_map/ppermute | solution.py:166
  9.5 0.5 %collective-permute-start = (bf16[944,128]{1,0:T(8,128)(2,1)S(1)}, bf16[944,128]{1,0:T(8,128)(2,1)S(1)}, u32[]{:S(2)}, u32[]{:S(2)}) collective-permute-start(bf16[944,128]{1,0:T(8,128)(2,1)S(1)} %get-tuple-element.21.refs_0_), channel_id=1, source_target_pairs={{0,2},{1,3},{2,0},{3,1},{4,6},{5,7},{6,4},{7,5},{8,10},{9,11},{10,... | collective-permute-start | bytes 725000 | tf_op jit(solution)/shard_map/ppermute | solution.py:166
  10.0 5.1 %collective-permute-done.2.refs_5_ = bf16[944,128]{1,0:T(8,128)(2,1)S(1)} collective-permute-done((bf16[944,128]{1,0:T(8,128)(2,1)S(1)}, bf16[944,128]{1,0:T(8,128)(2,1)S(1)}, u32[]{:S(2)}, u32[]{:S(2)}) %collective-permute-start.2) | collective-permute-done | bytes 241696 | tf_op jit(solution)/shard_map/ppermute | solution.py:166
  15.1 0.0 collective-permute-done.1.refs_3_
  15.1 2.6 %collective-permute-start.6 = (bf16[944,128]{1,0:T(8,128)(2,1)S(1)}, bf16[944,128]{1,0:T(8,128)(2,1)S(1)}, u32[]{:S(2)}, u32[]{:S(2)}) collective-permute-start(bf16[944,128]{1,0:T(8,128)(2,1)S(1)} %collective-permute-done.2.refs_5_), channel_id=1, source_target_pairs={{0,2},{1,3},{2,0},{3,1},{4,6},{5,7},{6,4},{7,5},{8,10},{9,11},{10,... | collective-permute-start | bytes 725000 | tf_op jit(solution)/shard_map/ppermute | solution.py:166
  17.7 1.5 %collective-permute-start.3 = (bf16[944,128]{1,0:T(8,128)(2,1)S(1)}, bf16[944,128]{1,0:T(8,128)(2,1)S(1)}, u32[]{:S(2)}, u32[]{:S(2)}) collective-permute-start(bf16[944,128]{1,0:T(8,128)(2,1)S(1)} %collective-permute-done.2.refs_5_), channel_id=1, source_target_pairs={{0,16},{1,17},{2,18},{3,19},{4,20},{5,21},{6,22},{7,23},{8,24},{9,... | collective-permute-start | bytes 725000 | tf_op jit(solution)/shard_map/ppermute | solution.py:166
  19.3 0.8 %collective-permute-done.4.refs_8_ = bf16[944,128]{1,0:T(8,128)(2,1)S(1)} collective-permute-done((bf16[944,128]{1,0:T(8,128)(2,1)S(1)}, bf16[944,128]{1,0:T(8,128)(2,1)S(1)}, u32[]{:S(2)}, u32[]{:S(2)}) %collective-permute-start.4) | collective-permute-done | bytes 241696 | tf_op jit(solution)/shard_map/ppermute | solution.py:166
  20.1 0.0 collective-permute-start.9
  20.1 0.6 %collective-permute-start.10 = (bf16[944,128]{1,0:T(8,128)(2,1)S(1)}, bf16[944,128]{1,0:T(8,128)(2,1)S(1)}, u32[]{:S(2)}, u32[]{:S(2)}) collective-permute-start(bf16[944,128]{1,0:T(8,128)(2,1)S(1)} %collective-permute-done.4.refs_8_), channel_id=1, source_target_pairs={{0,2},{1,3},{2,0},{3,1},{4,6},{5,7},{6,4},{7,5},{8,10},{9,11},{10,... | collective-permute-start | bytes 725000 | tf_op jit(solution)/shard_map/ppermute | solution.py:166
  20.7 3.0 %collective-permute-start.8 = (bf16[944,128]{1,0:T(8,128)(2,1)S(1)}, bf16[944,128]{1,0:T(8,128)(2,1)S(1)}, u32[]{:S(2)}, u32[]{:S(2)}) collective-permute-start(bf16[944,128]{1,0:T(8,128)(2,1)S(1)} %collective-permute-done.4.refs_8_), channel_id=1, source_target_pairs={{0,4},{1,5},{2,6},{3,7},{4,0},{5,1},{6,2},{7,3},{8,12},{9,13},{10,... | collective-permute-start | bytes 725000 | tf_op jit(solution)/shard_map/ppermute | solution.py:166
  23.6 0.9 %collective-permute-done.6.refs_7_ = bf16[944,128]{1,0:T(8,128)(2,1)S(1)} collective-permute-done((bf16[944,128]{1,0:T(8,128)(2,1)S(1)}, bf16[944,128]{1,0:T(8,128)(2,1)S(1)}, u32[]{:S(2)}, u32[]{:S(2)}) %collective-permute-start.6) | collective-permute-done | bytes 241696 | tf_op jit(solution)/shard_map/ppermute | solution.py:166
  24.5 0.0 collective-permute-done.3.refs_4_
  24.5 2.0 %collective-permute-start.5 = (bf16[944,128]{1,0:T(8,128)(2,1)S(1)}, bf16[944,128]{1,0:T(8,128)(2,1)S(1)}, u32[]{:S(2)}, u32[]{:S(2)}) collective-permute-start(bf16[944,128]{1,0:T(8,128)(2,1)S(1)} %collective-permute-done.3.refs_4_), channel_id=1, source_target_pairs={{0,2},{1,3},{2,0},{3,1},{4,6},{5,7},{6,4},{7,5},{8,10},{9,11},{10,... | collective-permute-start | bytes 725000 | tf_op jit(solution)/shard_map/ppermute | solution.py:166
  26.6 1.5 %collective-permute-start.7 = (bf16[944,128]{1,0:T(8,128)(2,1)S(1)}, bf16[944,128]{1,0:T(8,128)(2,1)S(1)}, u32[]{:S(2)}, u32[]{:S(2)}) collective-permute-start(bf16[944,128]{1,0:T(8,128)(2,1)S(1)} %collective-permute-done.4.refs_8_), channel_id=1, source_target_pairs={{0,16},{1,17},{2,18},{3,19},{4,20},{5,21},{6,22},{7,23},{8,24},{9,... | collective-permute-start | bytes 725000 | tf_op jit(solution)/shard_map/ppermute | solution.py:166
  28.1 3.6 %collective-permute-done.9.refs_11_ = bf16[944,128]{1,0:T(8,128)(2,1)S(1)} collective-permute-done((bf16[944,128]{1,0:T(8,128)(2,1)S(1)}, bf16[944,128]{1,0:T(8,128)(2,1)S(1)}, u32[]{:S(2)}, u32[]{:S(2)}) %collective-permute-start.9) | collective-permute-done | bytes 241696 | tf_op jit(solution)/shard_map/ppermute | solution.py:166
  31.6 0.0 collective-permute-start.11
  31.7 0.8 %collective-permute-start.12 = (bf16[944,128]{1,0:T(8,128)(2,1)S(1)}, bf16[944,128]{1,0:T(8,128)(2,1)S(1)}, u32[]{:S(2)}, u32[]{:S(2)}) collective-permute-start(bf16[944,128]{1,0:T(8,128)(2,1)S(1)} %collective-permute-done.9.refs_11_), channel_id=1, source_target_pairs={{0,2},{1,3},{2,0},{3,1},{4,6},{5,7},{6,4},{7,5},{8,10},{9,11},{10,... | collective-permute-start | bytes 725000 | tf_op jit(solution)/shard_map/ppermute | solution.py:166
  32.5 1.6 %collective-permute-start.13 = (bf16[944,128]{1,0:T(8,128)(2,1)S(1)}, bf16[944,128]{1,0:T(8,128)(2,1)S(1)}, u32[]{:S(2)}, u32[]{:S(2)}) collective-permute-start(bf16[944,128]{1,0:T(8,128)(2,1)S(1)} %collective-permute-done.10.refs_0_), channel_id=1, source_target_pairs={{0,16},{1,17},{2,18},{3,19},{4,20},{5,21},{6,22},{7,23},{8,24},{9,... | collective-permute-start | bytes 725000 | tf_op jit(solution)/shard_map/ppermute | solution.py:166
  34.1 0.0 collective-permute-done.5.refs_6_
  34.1 0.0 collective-permute-done.7.refs_9_
  34.1 2.3 %shard_map.56 = (f32[160,128]{1,0:T(8,128)S(1)}, f32[160,128]{1,0:T(8,128)S(1)}) custom-call(bf16[160,11008]{1,0:T(8,128)(2,1)S(1)} %bitcast.4, bf16[160,4096]{1,0:T(8,128)(2,1)S(1)} %bitcast.7, bf16[944,128]{1,0:T(8,128)(2,1)S(1)} %get-tuple-element.21.refs_0_, bf16[944,128]{1,0:T(8,128)(2,1)S(1)} %get-tuple-element.22.refs_1_, ...), custom_call_target="tpu_custom_call" | custom-call | flops 463994880 | bytes 6524928 | tf_op jit(solution)/shard_map/pallas_call | solution.py:191
  36.4 2.2 %collective-permute-done.11.refs_0_ = bf16[944,128]{1,0:T(8,128)(2,1)S(1)} collective-permute-done((bf16[944,128]{1,0:T(8,128)(2,1)S(1)}, bf16[944,128]{1,0:T(8,128)(2,1)S(1)}, u32[]{:S(2)}, u32[]{:S(2)}) %collective-permute-start.11) | collective-permute-done | bytes 241696 | tf_op jit(solution)/shard_map/ppermute | solution.py:166
  38.6 0.0 collective-permute-done.12.refs_1_
  38.6 0.4 shard_map.57
  39.0 0.0 collective-permute-done.13.refs_1_
  39.0 0.6 %shard_map.58 = (f32[32,80]{1,0:T(8,128)S(1)}, f32[32,80]{1,0:T(8,128)S(1)}) custom-call(bf16[160,11008]{1,0:T(8,128)(2,1)S(1)} %bitcast.6, bf16[160,4096]{1,0:T(8,128)(2,1)S(1)} %bitcast.9, f32[160,128]{1,0:T(8,128)S(1)} %get-tuple-element.32.in_ref, f32[160,128]{1,0:T(8,128)S(1)} %get-tuple-element.33.out_ref, ...), custom_call_target="tpu_custom_call" | custom-call | flops 77332480 | bytes 1087488 | tf_op jit(solution)/shard_map/pallas_call | solution.py:191
  39.7 0.0 collective-permute-start.14
  39.7 1.2 %collective-permute-done.14 = f32[32,80]{1,0:T(8,128)S(1)} collective-permute-done((f32[32,80]{1,0:T(8,128)S(1)}, f32[32,80]{1,0:T(8,128)S(1)}, u32[]{:S(2)}, u32[]{:S(2)}) %collective-permute-start.14) | collective-permute-done | bytes 10272 | tf_op jit(solution)/shard_map/ppermute | solution.py:166
  40.9 0.6 %add_bitcast_fusion = f32[80,32]{0,1:T(8,128)} fusion(f32[32,80]{1,0:T(8,128)S(1)} %get-tuple-element.35, f32[32,80]{1,0:T(8,128)S(1)} %collective-permute-done.14), kind=kLoop, calls=%fused_computation | loop fusion | flops 2560 | bytes 30720 | tf_op jit(solution)/shard_map/transpose | solution.py:208
  (7 shorter events, 0.0 us)
Async XLA Ops:
  0.0 34.1 %copy-start.1 = (bf16[1,160,4096]{2,1,0:T(8,128)(2,1)S(1)}, bf16[1,160,4096]{2,1,0:T(8,128)(2,1)}, u32[]{:S(2)}) copy-start(bf16[1,160,4096]{2,1,0:T(8,128)(2,1)} %param.6) | copy-start | bytes 3932164
  0.0 34.1 %copy-start = (bf16[1,160,11008]{2,1,0:T(8,128)(2,1)S(1)}, bf16[1,160,11008]{2,1,0:T(8,128)(2,1)}, u32[]{:S(2)}) copy-start(bf16[1,160,11008]{2,1,0:T(8,128)(2,1)} %param.5) | copy-start | bytes 10567684
  2.3 12.8 %collective-permute-start.2 = (bf16[944,128]{1,0:T(8,128)(2,1)S(1)}, bf16[944,128]{1,0:T(8,128)(2,1)S(1)}, u32[]{:S(2)}, u32[]{:S(2)}) collective-permute-start(bf16[944,128]{1,0:T(8,128)(2,1)S(1)} %get-tuple-element.22.refs_1_), channel_id=1, source_target_pairs={{0,4},{1,5},{2,6},{3,7},{4,0},{5,1},{6,2},{7,3},{8,12},{9,13},{10,... | collective-permute-start | bytes 725000 | tf_op jit(solution)/shard_map/ppermute | solution.py:166
  5.4 9.7 %collective-permute-start.1 = (bf16[944,128]{1,0:T(8,128)(2,1)S(1)}, bf16[944,128]{1,0:T(8,128)(2,1)S(1)}, u32[]{:S(2)}, u32[]{:S(2)}) collective-permute-start(bf16[944,128]{1,0:T(8,128)(2,1)S(1)} %get-tuple-element.22.refs_1_), channel_id=1, source_target_pairs={{0,2},{1,3},{2,0},{3,1},{4,6},{5,7},{6,4},{7,5},{8,10},{9,11},{10,... | collective-permute-start | bytes 725000 | tf_op jit(solution)/shard_map/ppermute | solution.py:166
  6.9 13.2 %collective-permute-start.4 = (bf16[944,128]{1,0:T(8,128)(2,1)S(1)}, bf16[944,128]{1,0:T(8,128)(2,1)S(1)}, u32[]{:S(2)}, u32[]{:S(2)}) collective-permute-start(bf16[944,128]{1,0:T(8,128)(2,1)S(1)} %get-tuple-element.21.refs_0_), channel_id=1, source_target_pairs={{0,8},{1,9},{2,10},{3,11},{4,12},{5,13},{6,14},{7,15},{8,0},{9,1},... | collective-permute-start | bytes 725000 | tf_op jit(solution)/shard_map/ppermute | solution.py:166
  9.5 11.2 %collective-permute-start = (bf16[944,128]{1,0:T(8,128)(2,1)S(1)}, bf16[944,128]{1,0:T(8,128)(2,1)S(1)}, u32[]{:S(2)}, u32[]{:S(2)}) collective-permute-start(bf16[944,128]{1,0:T(8,128)(2,1)S(1)} %get-tuple-element.21.refs_0_), channel_id=1, source_target_pairs={{0,2},{1,3},{2,0},{3,1},{4,6},{5,7},{6,4},{7,5},{8,10},{9,11},{10,... | collective-permute-start | bytes 725000 | tf_op jit(solution)/shard_map/ppermute | solution.py:166
  15.1 9.4 %collective-permute-start.6 = (bf16[944,128]{1,0:T(8,128)(2,1)S(1)}, bf16[944,128]{1,0:T(8,128)(2,1)S(1)}, u32[]{:S(2)}, u32[]{:S(2)}) collective-permute-start(bf16[944,128]{1,0:T(8,128)(2,1)S(1)} %collective-permute-done.2.refs_5_), channel_id=1, source_target_pairs={{0,2},{1,3},{2,0},{3,1},{4,6},{5,7},{6,4},{7,5},{8,10},{9,11},{10,... | collective-permute-start | bytes 725000 | tf_op jit(solution)/shard_map/ppermute | solution.py:166
  17.7 6.8 %collective-permute-start.3 = (bf16[944,128]{1,0:T(8,128)(2,1)S(1)}, bf16[944,128]{1,0:T(8,128)(2,1)S(1)}, u32[]{:S(2)}, u32[]{:S(2)}) collective-permute-start(bf16[944,128]{1,0:T(8,128)(2,1)S(1)} %collective-permute-done.2.refs_5_), channel_id=1, source_target_pairs={{0,16},{1,17},{2,18},{3,19},{4,20},{5,21},{6,22},{7,23},{8,24},{9,... | collective-permute-start | bytes 725000 | tf_op jit(solution)/shard_map/ppermute | solution.py:166
  20.1 11.6 %collective-permute-start.9 = (bf16[944,128]{1,0:T(8,128)(2,1)S(1)}, bf16[944,128]{1,0:T(8,128)(2,1)S(1)}, u32[]{:S(2)}, u32[]{:S(2)}) collective-permute-start(bf16[944,128]{1,0:T(8,128)(2,1)S(1)} %collective-permute-done.2.refs_5_), channel_id=1, source_target_pairs={{0,8},{1,9},{2,10},{3,11},{4,12},{5,13},{6,14},{7,15},{8,0},{9,1},... | collective-permute-start | bytes 725000 | tf_op jit(solution)/shard_map/ppermute | solution.py:166
  20.1 11.6 %collective-permute-start.10 = (bf16[944,128]{1,0:T(8,128)(2,1)S(1)}, bf16[944,128]{1,0:T(8,128)(2,1)S(1)}, u32[]{:S(2)}, u32[]{:S(2)}) collective-permute-start(bf16[944,128]{1,0:T(8,128)(2,1)S(1)} %collective-permute-done.4.refs_8_), channel_id=1, source_target_pairs={{0,2},{1,3},{2,0},{3,1},{4,6},{5,7},{6,4},{7,5},{8,10},{9,11},{10,... | collective-permute-start | bytes 725000 | tf_op jit(solution)/shard_map/ppermute | solution.py:166
  20.7 11.8 %collective-permute-start.8 = (bf16[944,128]{1,0:T(8,128)(2,1)S(1)}, bf16[944,128]{1,0:T(8,128)(2,1)S(1)}, u32[]{:S(2)}, u32[]{:S(2)}) collective-permute-start(bf16[944,128]{1,0:T(8,128)(2,1)S(1)} %collective-permute-done.4.refs_8_), channel_id=1, source_target_pairs={{0,4},{1,5},{2,6},{3,7},{4,0},{5,1},{6,2},{7,3},{8,12},{9,13},{10,... | collective-permute-start | bytes 725000 | tf_op jit(solution)/shard_map/ppermute | solution.py:166
  24.5 9.5 %collective-permute-start.5 = (bf16[944,128]{1,0:T(8,128)(2,1)S(1)}, bf16[944,128]{1,0:T(8,128)(2,1)S(1)}, u32[]{:S(2)}, u32[]{:S(2)}) collective-permute-start(bf16[944,128]{1,0:T(8,128)(2,1)S(1)} %collective-permute-done.3.refs_4_), channel_id=1, source_target_pairs={{0,2},{1,3},{2,0},{3,1},{4,6},{5,7},{6,4},{7,5},{8,10},{9,11},{10,... | collective-permute-start | bytes 725000 | tf_op jit(solution)/shard_map/ppermute | solution.py:166
  26.6 7.5 %collective-permute-start.7 = (bf16[944,128]{1,0:T(8,128)(2,1)S(1)}, bf16[944,128]{1,0:T(8,128)(2,1)S(1)}, u32[]{:S(2)}, u32[]{:S(2)}) collective-permute-start(bf16[944,128]{1,0:T(8,128)(2,1)S(1)} %collective-permute-done.4.refs_8_), channel_id=1, source_target_pairs={{0,16},{1,17},{2,18},{3,19},{4,20},{5,21},{6,22},{7,23},{8,24},{9,... | collective-permute-start | bytes 725000 | tf_op jit(solution)/shard_map/ppermute | solution.py:166
  31.6 7.0 %collective-permute-start.11 = (bf16[944,128]{1,0:T(8,128)(2,1)S(1)}, bf16[944,128]{1,0:T(8,128)(2,1)S(1)}, u32[]{:S(2)}, u32[]{:S(2)}) collective-permute-start(bf16[944,128]{1,0:T(8,128)(2,1)S(1)} %collective-permute-done.10.refs_0_), channel_id=1, source_target_pairs={{0,4},{1,5},{2,6},{3,7},{4,0},{5,1},{6,2},{7,3},{8,12},{9,13},{10,... | collective-permute-start | bytes 725000 | tf_op jit(solution)/shard_map/ppermute | solution.py:166
  31.7 7.0 %collective-permute-start.12 = (bf16[944,128]{1,0:T(8,128)(2,1)S(1)}, bf16[944,128]{1,0:T(8,128)(2,1)S(1)}, u32[]{:S(2)}, u32[]{:S(2)}) collective-permute-start(bf16[944,128]{1,0:T(8,128)(2,1)S(1)} %collective-permute-done.9.refs_11_), channel_id=1, source_target_pairs={{0,2},{1,3},{2,0},{3,1},{4,6},{5,7},{6,4},{7,5},{8,10},{9,11},{10,... | collective-permute-start | bytes 725000 | tf_op jit(solution)/shard_map/ppermute | solution.py:166
  32.5 6.6 %collective-permute-start.13 = (bf16[944,128]{1,0:T(8,128)(2,1)S(1)}, bf16[944,128]{1,0:T(8,128)(2,1)S(1)}, u32[]{:S(2)}, u32[]{:S(2)}) collective-permute-start(bf16[944,128]{1,0:T(8,128)(2,1)S(1)} %collective-permute-done.10.refs_0_), channel_id=1, source_target_pairs={{0,16},{1,17},{2,18},{3,19},{4,20},{5,21},{6,22},{7,23},{8,24},{9,... | collective-permute-start | bytes 725000 | tf_op jit(solution)/shard_map/ppermute | solution.py:166
  39.7 1.2 %collective-permute-start.14 = (f32[32,80]{1,0:T(8,128)S(1)}, f32[32,80]{1,0:T(8,128)S(1)}, u32[]{:S(2)}, u32[]{:S(2)}) collective-permute-start(f32[32,80]{1,0:T(8,128)S(1)} %get-tuple-element.36), channel_id=1, source_target_pairs={{0,1},{1,0},{2,3},{3,2},{4,5},{5,4},{6,7},{7,6},{8,9},{9,8},{10,11... | collective-permute-start | bytes 30728 | tf_op jit(solution)/shard_map/ppermute | solution.py:166

commit v4 on v3

--- a/solution.py
+++ b/solution.py
@@ -42,8 +42,8 @@
     ((1, 1, 1), (1, 0, 1), "x", ()),
     ((3, 0, 1), (1, 0, 1), 2, ()),
     ((1, 0, 0), (1, 0, 1), "y", ((0, 1, 1),)),
+    ((3, 0, 0), (2, 0, 0), 1, ((1, 0, 1), (0, 1, 1), (0, 1, 0),)),
     ((2, 1, 0), (2, 0, 0), "x", ((1, 0, 1), (0, 1, 1),)),
-    ((3, 0, 0), (2, 0, 0), 1, ((1, 0, 1), (0, 1, 1), (0, 1, 0),)),
     ((1, 1, 0), (1, 0, 0), "x", ((1, 0, 1), (0, 1, 1), (2, 0, 0), (0, 1, 0),)),
     ((2, 0, 1), (2, 0, 0), "y", ((1, 0, 1), (0, 1, 1), (0, 1, 0), (1, 0, 0), (1, 1, 1),)),
     ((3, 1, 0), (2, 1, 0), 1, ((1, 0, 1), (0, 1, 1), (2, 0, 0), (0, 1, 0), (1, 0, 0), (1, 1, 1),)),
@@ -57,11 +57,8 @@
 )
 
 
-def take_halves(half, ids_ref, in_ref, out_ref, first_ref, second_ref, ids, sems):
-    fetch = pltpu.make_async_copy(ids_ref, ids, sems.at[3])
-    fetch.start()
-    fetch.wait()
-    chosen = ids[lax.axis_index("layer")]
+def take_halves(half, ids_ref, in_ref, out_ref, first_ref, second_ref, sems):
+    chosen = ids_ref[lax.axis_index("layer")]
     part = lax.axis_index("parts")
     tail = in_ref.shape[1] - half
 
@@ -171,9 +168,9 @@
     have = dict(zip(((0, 0, 0), (0, 0, 1)), pl.pallas_call(
         functools.partial(take_halves, half),
         out_shape=(piece, piece),
-        in_specs=[pl.BlockSpec(memory_space=pl.ANY)] * 3,
+        in_specs=[pl.BlockSpec(memory_space=pltpu.SMEM)] + [pl.BlockSpec(memory_space=pl.ANY)] * 2,
         out_specs=[vmem] * 2,
-        scratch_shapes=[pltpu.SMEM(layer_ids.shape, layer_ids.dtype), pltpu.SemaphoreType.DMA((4,))],
+        scratch_shapes=[pltpu.SemaphoreType.DMA((3,))],
         compiler_params=pltpu.CompilerParams(vmem_limit_bytes=4 << 20),
     )(*in_hbm)))
     for arrives, passed_on, across, waits in MOVES:

time: 41.7 us -> 41.6 us (level)
  no operation moved by 1% of the time
where the time goes in v4:
time: 41.6 us; the launch traced here: 41.5 us
  starting transfers between devices  21.4 us (51%)
  waiting for transfers between devices  13.8 us (33%)
  Pallas kernels  5.62 us (14%)
  other arithmetic  0.61 us (1%)
    ppermute x15, starting transfers between devices, swap(): return lax.ppermute(value, AXES, pairs)  21.4 us
    ppermute x15, waiting for transfers between devices, swap(): return lax.ppermute(value, AXES, pairs)  13.8 us
    pallas_call x3, Pallas kernels, products(): pl.pallas_call(functools.partial(kernel, [z * x_size + x for z, x in bloc...  3.32 us
    pallas_call x1, Pallas kernels, swapped_form(): pl.pallas_call(functools.partial(take_halves, half), out_shape=(piece, pi...  2.3 us
  transfers between devices with their start and end apart: 15, of which 6 were waited for; matrix products, arithmetic and copies ran while one was open for 0% of the time, Pallas kernels for 7%

profile of v4, /device:TPU:0, one launch (start us, length us, event | category | flops | bytes accessed | tf_op | source)
XLA Modules:
  0.0 41.5 jit_solution(164585747584724973)
XLA Ops:
  0.0 2.3 %shard_map.55 = (bf16[944,128]{1,0:T(8,128)(2,1)S(1)}, bf16[944,128]{1,0:T(8,128)(2,1)S(1)}) custom-call(s32[32]{0:T(128)} %ids_ref.1, bf16[32,1376,128]{2,1,0:T(8,128)(2,1)} %in_ref.1, bf16[32,512,128]{2,1,0:T(8,128)(2,1)} %out_ref.1), custom_call_target="tpu_custom_call" | custom-call | tf_op jit(solution)/shard_map/pallas_call | solution.py:168
  2.3 3.1 %collective-permute-start.2 = (bf16[944,128]{1,0:T(8,128)(2,1)S(1)}, bf16[944,128]{1,0:T(8,128)(2,1)S(1)}, u32[]{:S(2)}, u32[]{:S(2)}) collective-permute-start(bf16[944,128]{1,0:T(8,128)(2,1)S(1)} %get-tuple-element.22.refs_1_), channel_id=1, source_target_pairs={{0,4},{1,5},{2,6},{3,7},{4,0},{5,1},{6,2},{7,3},{8,12},{9,13},{10,... | collective-permute-start | bytes 725000 | tf_op jit(solution)/shard_map/ppermute | solution.py:163
  5.4 1.5 %collective-permute-start.1 = (bf16[944,128]{1,0:T(8,128)(2,1)S(1)}, bf16[944,128]{1,0:T(8,128)(2,1)S(1)}, u32[]{:S(2)}, u32[]{:S(2)}) collective-permute-start(bf16[944,128]{1,0:T(8,128)(2,1)S(1)} %get-tuple-element.22.refs_1_), channel_id=1, source_target_pairs={{0,2},{1,3},{2,0},{3,1},{4,6},{5,7},{6,4},{7,5},{8,10},{9,11},{10,... | collective-permute-start | bytes 725000 | tf_op jit(solution)/shard_map/ppermute | solution.py:163
  6.9 2.6 %collective-permute-start.4 = (bf16[944,128]{1,0:T(8,128)(2,1)S(1)}, bf16[944,128]{1,0:T(8,128)(2,1)S(1)}, u32[]{:S(2)}, u32[]{:S(2)}) collective-permute-start(bf16[944,128]{1,0:T(8,128)(2,1)S(1)} %get-tuple-element.21.refs_0_), channel_id=1, source_target_pairs={{0,8},{1,9},{2,10},{3,11},{4,12},{5,13},{6,14},{7,15},{8,0},{9,1},... | collective-permute-start | bytes 725000 | tf_op jit(solution)/shard_map/ppermute | solution.py:163
  9.5 0.5 %collective-permute-start = (bf16[944,128]{1,0:T(8,128)(2,1)S(1)}, bf16[944,128]{1,0:T(8,128)(2,1)S(1)}, u32[]{:S(2)}, u32[]{:S(2)}) collective-permute-start(bf16[944,128]{1,0:T(8,128)(2,1)S(1)} %get-tuple-element.21.refs_0_), channel_id=1, source_target_pairs={{0,2},{1,3},{2,0},{3,1},{4,6},{5,7},{6,4},{7,5},{8,10},{9,11},{10,... | collective-permute-start | bytes 725000 | tf_op jit(solution)/shard_map/ppermute | solution.py:163
  10.0 5.1 %collective-permute-done.2.refs_5_ = bf16[944,128]{1,0:T(8,128)(2,1)S(1)} collective-permute-done((bf16[944,128]{1,0:T(8,128)(2,1)S(1)}, bf16[944,128]{1,0:T(8,128)(2,1)S(1)}, u32[]{:S(2)}, u32[]{:S(2)}) %collective-permute-start.2) | collective-permute-done | bytes 241696 | tf_op jit(solution)/shard_map/ppermute | solution.py:163
  15.1 0.0 collective-permute-done.1.refs_3_
  15.1 2.6 %collective-permute-start.6 = (bf16[944,128]{1,0:T(8,128)(2,1)S(1)}, bf16[944,128]{1,0:T(8,128)(2,1)S(1)}, u32[]{:S(2)}, u32[]{:S(2)}) collective-permute-start(bf16[944,128]{1,0:T(8,128)(2,1)S(1)} %collective-permute-done.2.refs_5_), channel_id=1, source_target_pairs={{0,2},{1,3},{2,0},{3,1},{4,6},{5,7},{6,4},{7,5},{8,10},{9,11},{10,... | collective-permute-start | bytes 725000 | tf_op jit(solution)/shard_map/ppermute | solution.py:163
  17.7 1.5 %collective-permute-start.3 = (bf16[944,128]{1,0:T(8,128)(2,1)S(1)}, bf16[944,128]{1,0:T(8,128)(2,1)S(1)}, u32[]{:S(2)}, u32[]{:S(2)}) collective-permute-start(bf16[944,128]{1,0:T(8,128)(2,1)S(1)} %collective-permute-done.2.refs_5_), channel_id=1, source_target_pairs={{0,16},{1,17},{2,18},{3,19},{4,20},{5,21},{6,22},{7,23},{8,24},{9,... | collective-permute-start | bytes 725000 | tf_op jit(solution)/shard_map/ppermute | solution.py:163
  19.3 0.8 %collective-permute-done.4.refs_8_ = bf16[944,128]{1,0:T(8,128)(2,1)S(1)} collective-permute-done((bf16[944,128]{1,0:T(8,128)(2,1)S(1)}, bf16[944,128]{1,0:T(8,128)(2,1)S(1)}, u32[]{:S(2)}, u32[]{:S(2)}) %collective-permute-start.4) | collective-permute-done | bytes 241696 | tf_op jit(solution)/shard_map/ppermute | solution.py:163
  20.1 0.0 collective-permute-start.9
  20.1 0.6 %collective-permute-start.10 = (bf16[944,128]{1,0:T(8,128)(2,1)S(1)}, bf16[944,128]{1,0:T(8,128)(2,1)S(1)}, u32[]{:S(2)}, u32[]{:S(2)}) collective-permute-start(bf16[944,128]{1,0:T(8,128)(2,1)S(1)} %collective-permute-done.4.refs_8_), channel_id=1, source_target_pairs={{0,2},{1,3},{2,0},{3,1},{4,6},{5,7},{6,4},{7,5},{8,10},{9,11},{10,... | collective-permute-start | bytes 725000 | tf_op jit(solution)/shard_map/ppermute | solution.py:163
  20.7 3.0 %collective-permute-start.8 = (bf16[944,128]{1,0:T(8,128)(2,1)S(1)}, bf16[944,128]{1,0:T(8,128)(2,1)S(1)}, u32[]{:S(2)}, u32[]{:S(2)}) collective-permute-start(bf16[944,128]{1,0:T(8,128)(2,1)S(1)} %collective-permute-done.4.refs_8_), channel_id=1, source_target_pairs={{0,4},{1,5},{2,6},{3,7},{4,0},{5,1},{6,2},{7,3},{8,12},{9,13},{10,... | collective-permute-start | bytes 725000 | tf_op jit(solution)/shard_map/ppermute | solution.py:163
  23.6 0.9 %collective-permute-done.6.refs_7_ = bf16[944,128]{1,0:T(8,128)(2,1)S(1)} collective-permute-done((bf16[944,128]{1,0:T(8,128)(2,1)S(1)}, bf16[944,128]{1,0:T(8,128)(2,1)S(1)}, u32[]{:S(2)}, u32[]{:S(2)}) %collective-permute-start.6) | collective-permute-done | bytes 241696 | tf_op jit(solution)/shard_map/ppermute | solution.py:163
  24.5 0.0 collective-permute-done.3.refs_4_
  24.5 2.0 %collective-permute-start.5 = (bf16[944,128]{1,0:T(8,128)(2,1)S(1)}, bf16[944,128]{1,0:T(8,128)(2,1)S(1)}, u32[]{:S(2)}, u32[]{:S(2)}) collective-permute-start(bf16[944,128]{1,0:T(8,128)(2,1)S(1)} %collective-permute-done.3.refs_4_), channel_id=1, source_target_pairs={{0,2},{1,3},{2,0},{3,1},{4,6},{5,7},{6,4},{7,5},{8,10},{9,11},{10,... | collective-permute-start | bytes 725000 | tf_op jit(solution)/shard_map/ppermute | solution.py:163
  26.6 1.5 %collective-permute-start.7 = (bf16[944,128]{1,0:T(8,128)(2,1)S(1)}, bf16[944,128]{1,0:T(8,128)(2,1)S(1)}, u32[]{:S(2)}, u32[]{:S(2)}) collective-permute-start(bf16[944,128]{1,0:T(8,128)(2,1)S(1)} %collective-permute-done.4.refs_8_), channel_id=1, source_target_pairs={{0,16},{1,17},{2,18},{3,19},{4,20},{5,21},{6,22},{7,23},{8,24},{9,... | collective-permute-start | bytes 725000 | tf_op jit(solution)/shard_map/ppermute | solution.py:163
  28.1 3.6 %collective-permute-done.9.refs_11_ = bf16[944,128]{1,0:T(8,128)(2,1)S(1)} collective-permute-done((bf16[944,128]{1,0:T(8,128)(2,1)S(1)}, bf16[944,128]{1,0:T(8,128)(2,1)S(1)}, u32[]{:S(2)}, u32[]{:S(2)}) %collective-permute-start.9) | collective-permute-done | bytes 241696 | tf_op jit(solution)/shard_map/ppermute | solution.py:163
  31.6 0.0 collective-permute-start.11
  31.7 0.8 %collective-permute-start.12 = (bf16[944,128]{1,0:T(8,128)(2,1)S(1)}, bf16[944,128]{1,0:T(8,128)(2,1)S(1)}, u32[]{:S(2)}, u32[]{:S(2)}) collective-permute-start(bf16[944,128]{1,0:T(8,128)(2,1)S(1)} %collective-permute-done.9.refs_11_), channel_id=1, source_target_pairs={{0,2},{1,3},{2,0},{3,1},{4,6},{5,7},{6,4},{7,5},{8,10},{9,11},{10,... | collective-permute-start | bytes 725000 | tf_op jit(solution)/shard_map/ppermute | solution.py:163
  32.4 1.6 %collective-permute-start.13 = (bf16[944,128]{1,0:T(8,128)(2,1)S(1)}, bf16[944,128]{1,0:T(8,128)(2,1)S(1)}, u32[]{:S(2)}, u32[]{:S(2)}) collective-permute-start(bf16[944,128]{1,0:T(8,128)(2,1)S(1)} %collective-permute-done.10.refs_0_), channel_id=1, source_target_pairs={{0,16},{1,17},{2,18},{3,19},{4,20},{5,21},{6,22},{7,23},{8,24},{9,... | collective-permute-start | bytes 725000 | tf_op jit(solution)/shard_map/ppermute | solution.py:163
  34.1 0.0 collective-permute-done.5.refs_6_
  34.1 0.0 collective-permute-done.7.refs_9_
  34.1 2.3 %shard_map.56 = (f32[160,128]{1,0:T(8,128)S(1)}, f32[160,128]{1,0:T(8,128)S(1)}) custom-call(bf16[160,11008]{1,0:T(8,128)(2,1)S(1)} %bitcast.4, bf16[160,4096]{1,0:T(8,128)(2,1)S(1)} %bitcast.7, bf16[944,128]{1,0:T(8,128)(2,1)S(1)} %get-tuple-element.21.refs_0_, bf16[944,128]{1,0:T(8,128)(2,1)S(1)} %get-tuple-element.22.refs_1_, ...), custom_call_target="tpu_custom_call" | custom-call | flops 463994880 | bytes 6524928 | tf_op jit(solution)/shard_map/pallas_call | solution.py:188
  36.4 2.2 %collective-permute-done.11.refs_0_ = bf16[944,128]{1,0:T(8,128)(2,1)S(1)} collective-permute-done((bf16[944,128]{1,0:T(8,128)(2,1)S(1)}, bf16[944,128]{1,0:T(8,128)(2,1)S(1)}, u32[]{:S(2)}, u32[]{:S(2)}) %collective-permute-start.11) | collective-permute-done | bytes 241696 | tf_op jit(solution)/shard_map/ppermute | solution.py:163
  38.6 0.0 collective-permute-done.12.refs_1_
  38.6 0.4 shard_map.57
  39.0 0.0 collective-permute-done.13.refs_1_
  39.0 0.6 %shard_map.58 = (f32[32,80]{1,0:T(8,128)S(1)}, f32[32,80]{1,0:T(8,128)S(1)}) custom-call(bf16[160,11008]{1,0:T(8,128)(2,1)S(1)} %bitcast.6, bf16[160,4096]{1,0:T(8,128)(2,1)S(1)} %bitcast.9, f32[160,128]{1,0:T(8,128)S(1)} %get-tuple-element.32.in_ref, f32[160,128]{1,0:T(8,128)S(1)} %get-tuple-element.33.out_ref, ...), custom_call_target="tpu_custom_call" | custom-call | flops 77332480 | bytes 1087488 | tf_op jit(solution)/shard_map/pallas_call | solution.py:188
  39.7 0.0 collective-permute-start.14
  39.7 1.2 %collective-permute-done.14 = f32[32,80]{1,0:T(8,128)S(1)} collective-permute-done((f32[32,80]{1,0:T(8,128)S(1)}, f32[32,80]{1,0:T(8,128)S(1)}, u32[]{:S(2)}, u32[]{:S(2)}) %collective-permute-start.14) | collective-permute-done | bytes 10272 | tf_op jit(solution)/shard_map/ppermute | solution.py:163
  40.9 0.6 %add_bitcast_fusion = f32[80,32]{0,1:T(8,128)} fusion(f32[32,80]{1,0:T(8,128)S(1)} %get-tuple-element.35, f32[32,80]{1,0:T(8,128)S(1)} %collective-permute-done.14), kind=kLoop, calls=%fused_computation | loop fusion | flops 2560 | bytes 30720 | tf_op jit(solution)/shard_map/transpose | solution.py:205
  (7 shorter events, 0.0 us)
Async XLA Ops:
  0.0 34.1 %copy-start.1 = (bf16[1,160,4096]{2,1,0:T(8,128)(2,1)S(1)}, bf16[1,160,4096]{2,1,0:T(8,128)(2,1)}, u32[]{:S(2)}) copy-start(bf16[1,160,4096]{2,1,0:T(8,128)(2,1)} %param.6) | copy-start | bytes 3932164
  0.0 34.1 %copy-start = (bf16[1,160,11008]{2,1,0:T(8,128)(2,1)S(1)}, bf16[1,160,11008]{2,1,0:T(8,128)(2,1)}, u32[]{:S(2)}) copy-start(bf16[1,160,11008]{2,1,0:T(8,128)(2,1)} %param.5) | copy-start | bytes 10567684
  2.3 12.8 %collective-permute-start.2 = (bf16[944,128]{1,0:T(8,128)(2,1)S(1)}, bf16[944,128]{1,0:T(8,128)(2,1)S(1)}, u32[]{:S(2)}, u32[]{:S(2)}) collective-permute-start(bf16[944,128]{1,0:T(8,128)(2,1)S(1)} %get-tuple-element.22.refs_1_), channel_id=1, source_target_pairs={{0,4},{1,5},{2,6},{3,7},{4,0},{5,1},{6,2},{7,3},{8,12},{9,13},{10,... | collective-permute-start | bytes 725000 | tf_op jit(solution)/shard_map/ppermute | solution.py:163
  5.4 9.7 %collective-permute-start.1 = (bf16[944,128]{1,0:T(8,128)(2,1)S(1)}, bf16[944,128]{1,0:T(8,128)(2,1)S(1)}, u32[]{:S(2)}, u32[]{:S(2)}) collective-permute-start(bf16[944,128]{1,0:T(8,128)(2,1)S(1)} %get-tuple-element.22.refs_1_), channel_id=1, source_target_pairs={{0,2},{1,3},{2,0},{3,1},{4,6},{5,7},{6,4},{7,5},{8,10},{9,11},{10,... | collective-permute-start | bytes 725000 | tf_op jit(solution)/shard_map/ppermute | solution.py:163
  6.9 13.2 %collective-permute-start.4 = (bf16[944,128]{1,0:T(8,128)(2,1)S(1)}, bf16[944,128]{1,0:T(8,128)(2,1)S(1)}, u32[]{:S(2)}, u32[]{:S(2)}) collective-permute-start(bf16[944,128]{1,0:T(8,128)(2,1)S(1)} %get-tuple-element.21.refs_0_), channel_id=1, source_target_pairs={{0,8},{1,9},{2,10},{3,11},{4,12},{5,13},{6,14},{7,15},{8,0},{9,1},... | collective-permute-start | bytes 725000 | tf_op jit(solution)/shard_map/ppermute | solution.py:163
  9.5 11.2 %collective-permute-start = (bf16[944,128]{1,0:T(8,128)(2,1)S(1)}, bf16[944,128]{1,0:T(8,128)(2,1)S(1)}, u32[]{:S(2)}, u32[]{:S(2)}) collective-permute-start(bf16[944,128]{1,0:T(8,128)(2,1)S(1)} %get-tuple-element.21.refs_0_), channel_id=1, source_target_pairs={{0,2},{1,3},{2,0},{3,1},{4,6},{5,7},{6,4},{7,5},{8,10},{9,11},{10,... | collective-permute-start | bytes 725000 | tf_op jit(solution)/shard_map/ppermute | solution.py:163
  15.1 9.4 %collective-permute-start.6 = (bf16[944,128]{1,0:T(8,128)(2,1)S(1)}, bf16[944,128]{1,0:T(8,128)(2,1)S(1)}, u32[]{:S(2)}, u32[]{:S(2)}) collective-permute-start(bf16[944,128]{1,0:T(8,128)(2,1)S(1)} %collective-permute-done.2.refs_5_), channel_id=1, source_target_pairs={{0,2},{1,3},{2,0},{3,1},{4,6},{5,7},{6,4},{7,5},{8,10},{9,11},{10,... | collective-permute-start | bytes 725000 | tf_op jit(solution)/shard_map/ppermute | solution.py:163
  17.7 6.8 %collective-permute-start.3 = (bf16[944,128]{1,0:T(8,128)(2,1)S(1)}, bf16[944,128]{1,0:T(8,128)(2,1)S(1)}, u32[]{:S(2)}, u32[]{:S(2)}) collective-permute-start(bf16[944,128]{1,0:T(8,128)(2,1)S(1)} %collective-permute-done.2.refs_5_), channel_id=1, source_target_pairs={{0,16},{1,17},{2,18},{3,19},{4,20},{5,21},{6,22},{7,23},{8,24},{9,... | collective-permute-start | bytes 725000 | tf_op jit(solution)/shard_map/ppermute | solution.py:163
  20.1 11.6 %collective-permute-start.9 = (bf16[944,128]{1,0:T(8,128)(2,1)S(1)}, bf16[944,128]{1,0:T(8,128)(2,1)S(1)}, u32[]{:S(2)}, u32[]{:S(2)}) collective-permute-start(bf16[944,128]{1,0:T(8,128)(2,1)S(1)} %collective-permute-done.2.refs_5_), channel_id=1, source_target_pairs={{0,8},{1,9},{2,10},{3,11},{4,12},{5,13},{6,14},{7,15},{8,0},{9,1},... | collective-permute-start | bytes 725000 | tf_op jit(solution)/shard_map/ppermute | solution.py:163
  20.1 11.6 %collective-permute-start.10 = (bf16[944,128]{1,0:T(8,128)(2,1)S(1)}, bf16[944,128]{1,0:T(8,128)(2,1)S(1)}, u32[]{:S(2)}, u32[]{:S(2)}) collective-permute-start(bf16[944,128]{1,0:T(8,128)(2,1)S(1)} %collective-permute-done.4.refs_8_), channel_id=1, source_target_pairs={{0,2},{1,3},{2,0},{3,1},{4,6},{5,7},{6,4},{7,5},{8,10},{9,11},{10,... | collective-permute-start | bytes 725000 | tf_op jit(solution)/shard_map/ppermute | solution.py:163
  20.7 11.8 %collective-permute-start.8 = (bf16[944,128]{1,0:T(8,128)(2,1)S(1)}, bf16[944,128]{1,0:T(8,128)(2,1)S(1)}, u32[]{:S(2)}, u32[]{:S(2)}) collective-permute-start(bf16[944,128]{1,0:T(8,128)(2,1)S(1)} %collective-permute-done.4.refs_8_), channel_id=1, source_target_pairs={{0,4},{1,5},{2,6},{3,7},{4,0},{5,1},{6,2},{7,3},{8,12},{9,13},{10,... | collective-permute-start | bytes 725000 | tf_op jit(solution)/shard_map/ppermute | solution.py:163
  24.5 9.5 %collective-permute-start.5 = (bf16[944,128]{1,0:T(8,128)(2,1)S(1)}, bf16[944,128]{1,0:T(8,128)(2,1)S(1)}, u32[]{:S(2)}, u32[]{:S(2)}) collective-permute-start(bf16[944,128]{1,0:T(8,128)(2,1)S(1)} %collective-permute-done.3.refs_4_), channel_id=1, source_target_pairs={{0,2},{1,3},{2,0},{3,1},{4,6},{5,7},{6,4},{7,5},{8,10},{9,11},{10,... | collective-permute-start | bytes 725000 | tf_op jit(solution)/shard_map/ppermute | solution.py:163
  26.6 7.5 %collective-permute-start.7 = (bf16[944,128]{1,0:T(8,128)(2,1)S(1)}, bf16[944,128]{1,0:T(8,128)(2,1)S(1)}, u32[]{:S(2)}, u32[]{:S(2)}) collective-permute-start(bf16[944,128]{1,0:T(8,128)(2,1)S(1)} %collective-permute-done.4.refs_8_), channel_id=1, source_target_pairs={{0,16},{1,17},{2,18},{3,19},{4,20},{5,21},{6,22},{7,23},{8,24},{9,... | collective-permute-start | bytes 725000 | tf_op jit(solution)/shard_map/ppermute | solution.py:163
  31.6 7.0 %collective-permute-start.11 = (bf16[944,128]{1,0:T(8,128)(2,1)S(1)}, bf16[944,128]{1,0:T(8,128)(2,1)S(1)}, u32[]{:S(2)}, u32[]{:S(2)}) collective-permute-start(bf16[944,128]{1,0:T(8,128)(2,1)S(1)} %collective-permute-done.10.refs_0_), channel_id=1, source_target_pairs={{0,4},{1,5},{2,6},{3,7},{4,0},{5,1},{6,2},{7,3},{8,12},{9,13},{10,... | collective-permute-start | bytes 725000 | tf_op jit(solution)/shard_map/ppermute | solution.py:163
  31.7 7.0 %collective-permute-start.12 = (bf16[944,128]{1,0:T(8,128)(2,1)S(1)}, bf16[944,128]{1,0:T(8,128)(2,1)S(1)}, u32[]{:S(2)}, u32[]{:S(2)}) collective-permute-start(bf16[944,128]{1,0:T(8,128)(2,1)S(1)} %collective-permute-done.9.refs_11_), channel_id=1, source_target_pairs={{0,2},{1,3},{2,0},{3,1},{4,6},{5,7},{6,4},{7,5},{8,10},{9,11},{10,... | collective-permute-start | bytes 725000 | tf_op jit(solution)/shard_map/ppermute | solution.py:163
  32.4 6.6 %collective-permute-start.13 = (bf16[944,128]{1,0:T(8,128)(2,1)S(1)}, bf16[944,128]{1,0:T(8,128)(2,1)S(1)}, u32[]{:S(2)}, u32[]{:S(2)}) collective-permute-start(bf16[944,128]{1,0:T(8,128)(2,1)S(1)} %collective-permute-done.10.refs_0_), channel_id=1, source_target_pairs={{0,16},{1,17},{2,18},{3,19},{4,20},{5,21},{6,22},{7,23},{8,24},{9,... | collective-permute-start | bytes 725000 | tf_op jit(solution)/shard_map/ppermute | solution.py:163
  39.7 1.2 %collective-permute-start.14 = (f32[32,80]{1,0:T(8,128)S(1)}, f32[32,80]{1,0:T(8,128)S(1)}, u32[]{:S(2)}, u32[]{:S(2)}) collective-permute-start(f32[32,80]{1,0:T(8,128)S(1)} %get-tuple-element.36), channel_id=1, source_target_pairs={{0,1},{1,0},{2,3},{3,2},{4,5},{5,4},{6,7},{7,6},{8,9},{9,8},{10,11... | collective-permute-start | bytes 30728 | tf_op jit(solution)/shard_map/ppermute | solution.py:163
